TPU v7x, 256 devices: a whole 4x4x8 slice. The times are simulated.
256 devices in a mesh: fsdp: 64 (over y, z, core), tp: 4 (over x).
Axes of the slice: x: 4, y: 4, z: 8, core: 2. Of those that a mesh axis runs over, the one named last changes fastest.
Arguments:
- momentum: float32 [18432, 7168], P('fsdp', 'tp'), may hold values from -120 to 120
- gradient: bfloat16 [18432, 7168], P('fsdp', 'tp'), may hold values from -4 to 4
- column_basis: bfloat16 [7168, 896], P('tp'), may hold values from -0.0625 to 0.0625
Outputs:
- momentum_new: float32 [18432, 7168], P('fsdp', 'tp')
- update: bfloat16 [18432, 7168], P('fsdp', 'tp')
- new_basis: bfloat16 [7168, 896], P('tp')
All inputs are finite; a program needn't handle non-finite values.
Results may differ from a plain program's by a relative error of at most 0.007.
Values may be sent and summed in bfloat16 or wider, within the bound.
A program may use at most 128 MiB of HBM per device.

v0:
```python
import math

import jax
import jax.numpy as jnp
from jax import lax
from jax.sharding import PartitionSpec as P

ROWS_FF = 18432
COLS_D = 7168
RANK = 896


RIDGE = 0.001
DECAY = 0.8
EPS = 1e-06


def cross_terms(left_rows, other_rows):
    return lax.dot_general(
        left_rows,
        other_rows,
        (((0,), (0,)), ((), ())),
        precision=lax.Precision.HIGHEST,
        preferred_element_type=jnp.float32,
    )


def gram_payload(projected):
    payload = cross_terms(projected, projected)
    return payload


def gram_matrix(summed, rank_size):
    return summed + RIDGE * jnp.eye(rank_size, dtype=jnp.float32)


def solve_rows(lower_factor, rows_in):
    return lax.linalg.triangular_solve(
        lower_factor, rows_in, left_side=False, lower=True, transpose_a=True
    )


def body(momentum, gradient, column_basis):
    blended = momentum + gradient.astype(jnp.float32)
    blended_low = blended.astype(jnp.bfloat16)
    partial_proj = jnp.dot(blended_low, column_basis, preferred_element_type=jnp.float32)
    rank_size = column_basis.shape[1]
    projected = lax.psum(partial_proj, "tp")
    summed = lax.psum(gram_payload(projected), "fsdp")
    lower_factor = jnp.linalg.cholesky(gram_matrix(summed, rank_size))
    orthonormal = solve_rows(lower_factor, projected)
    ortho_low = orthonormal.astype(jnp.bfloat16)
    right_factor = lax.psum_scatter(
        lax.dot_general(
            blended_low, ortho_low, (((0,), (0,)), ((), ())), preferred_element_type=jnp.float32
        ),
        "fsdp",
        scatter_dimension=0,
        tiled=True,
    )
    squares_sum = lax.psum(jnp.sum(right_factor * right_factor, axis=0), ("fsdp", "tp"))
    column_rms = jnp.sqrt(squares_sum / COLS_D + EPS)
    basis_piece = (right_factor / column_rms).astype(jnp.bfloat16)
    new_basis = lax.all_gather(basis_piece, "fsdp", axis=0, tiled=True)
    feed_low = (orthonormal * column_rms).astype(jnp.bfloat16)
    stacked = jnp.concatenate([feed_low, ortho_low], axis=0)
    products = lax.dot_general(
        stacked, new_basis, (((1,), (1,)), ((), ())), preferred_element_type=jnp.float32
    )
    rows_here = momentum.shape[0]
    momentum_new = blended - (1.0 - DECAY) * products[:rows_here]
    update = (math.sqrt(ROWS_FF / RANK) * products[rows_here:]).astype(jnp.bfloat16)
    return (momentum_new, update, new_basis)


def solution(mesh):
    placed = (P("fsdp", "tp"), P("fsdp", "tp"), P("tp", None))
    return jax.shard_map(
        body,
        mesh=mesh,
        in_specs=placed,
        out_specs=(P("fsdp", "tp"), P("fsdp", "tp"), P("tp", None)),
        check_vma=False,
    )
```

profile of v0, /device:TPU:1, one launch (start us, length us, event | category | flops | bytes accessed | tf_op | source)
XLA Modules:
  0.0 970.8 jit_solution(223382043075072282)
XLA Ops:
  13.2 53.4 %all-reduce.6.cloned.1.call-done = f32[288,896]{1,0:T(8,128)} async-done(((f32[288,896]{1,0:T(8,128)}), f32[288,896]{1,0:T(8,128)}) %all-reduce.6.cloned.1.call-update) | async-done | bytes 1032208 | tf_op jit(solution)/shard_map/psum | solution.py:48
  66.6 8.9 fusion.70
  76.1 193.0 %all-reduce.8.cloned.1.call-done = f32[896,896]{0,1:T(8,128)} async-done(((f32[896,896]{0,1:T(8,128)}), f32[896,896]{0,1:T(8,128)}) %all-reduce.8.cloned.1.call-update) | async-done | bytes 3211280 | tf_op jit(solution)/shard_map/psum | solution.py:49
  282.4 11.7 %cholesky.194 = f32[128,128]{1,0:T(8,128)S(1)} custom-call(f32[128,128]{1,0:T(8,128)S(1)} %cholesky.499), custom_call_target="Cholesky" | custom-call | tf_op jit(solution)/shard_map/jit(cholesky)/cholesky | solution.py:50
  294.3 9.8 %custom-call.54 = f32[1,128,128]{1,2,0:T(8,128)S(1)} custom-call(f32[1,128,128]{2,1,0:T(8,128)S(1)} %get-tuple-element.63), custom_call_target="InvertDiagBlocksLowerTriangular" | custom-call | tf_op jit(solution)/shard_map/jit(cholesky)/cholesky | solution.py:50
  310.6 11.7 %cholesky.215 = f32[128,128]{1,0:T(8,128)S(1)} custom-call(f32[128,128]{1,0:T(8,128)S(1)} %cholesky.503), custom_call_target="Cholesky" | custom-call | tf_op jit(solution)/shard_map/jit(cholesky)/cholesky | solution.py:50
  322.4 10.3 %custom-call.55 = f32[1,128,128]{1,2,0:T(8,128)S(1)} custom-call(f32[1,128,128]{2,1,0:T(8,128)S(1)} %get-tuple-element.61), custom_call_target="InvertDiagBlocksLowerTriangular" | custom-call | tf_op jit(solution)/shard_map/jit(cholesky)/cholesky | solution.py:50
  338.9 13.2 %cholesky.409 = f32[128,128]{1,0:T(8,128)} custom-call(f32[128,128]{1,0:T(8,128)} %cholesky.508), custom_call_target="Cholesky" | custom-call | tf_op jit(solution)/shard_map/jit(cholesky)/cholesky | solution.py:50
  356.5 11.3 %custom-call.56 = f32[1,128,128]{1,2,0:T(8,128)} custom-call(f32[1,128,128]{2,1,0:T(8,128)} %get-tuple-element.59), custom_call_target="InvertDiagBlocksLowerTriangular" | custom-call | tf_op jit(solution)/shard_map/jit(cholesky)/cholesky | solution.py:50
  372.6 12.5 %cholesky.428 = f32[128,128]{1,0:T(8,128)} custom-call(f32[128,128]{1,0:T(8,128)S(1)} %cholesky.513), custom_call_target="Cholesky" | custom-call | tf_op jit(solution)/shard_map/jit(cholesky)/cholesky | solution.py:50
  388.1 10.6 %custom-call.57 = f32[1,128,128]{1,2,0:T(8,128)S(1)} custom-call(f32[1,128,128]{2,1,0:T(8,128)} %get-tuple-element.57), custom_call_target="InvertDiagBlocksLowerTriangular" | custom-call | tf_op jit(solution)/shard_map/jit(cholesky)/cholesky | solution.py:50
  402.6 11.7 %cholesky.447 = f32[128,128]{1,0:T(8,128)S(1)} custom-call(f32[128,128]{1,0:T(8,128)S(1)} %cholesky.518), custom_call_target="Cholesky" | custom-call | tf_op jit(solution)/shard_map/jit(cholesky)/cholesky | solution.py:50
  416.2 10.8 %custom-call.58 = f32[1,128,128]{1,2,0:T(8,128)S(1)} custom-call(f32[1,128,128]{2,1,0:T(8,128)} %get-tuple-element.55), custom_call_target="InvertDiagBlocksLowerTriangular" | custom-call | tf_op jit(solution)/shard_map/jit(cholesky)/cholesky | solution.py:50
  430.5 11.7 %cholesky.467 = f32[128,128]{1,0:T(8,128)S(1)} custom-call(f32[128,128]{1,0:T(8,128)S(1)} %cholesky.523), custom_call_target="Cholesky" | custom-call | tf_op jit(solution)/shard_map/jit(cholesky)/cholesky | solution.py:50
  443.6 9.8 %custom-call.59 = f32[1,128,128]{1,2,0:T(8,128)S(1)} custom-call(f32[1,128,128]{2,1,0:T(8,128)S(1)} %get-tuple-element.53), custom_call_target="InvertDiagBlocksLowerTriangular" | custom-call | tf_op jit(solution)/shard_map/jit(cholesky)/cholesky | solution.py:50
  456.3 12.1 %cholesky.485 = f32[128,128]{1,0:T(8,128)S(1)} custom-call(f32[128,128]{1,0:T(8,128)S(1)} %convolution_subtract_fusion.11), custom_call_target="Cholesky" | custom-call | tf_op jit(solution)/shard_map/jit(cholesky)/cholesky | solution.py:50
  482.5 26.2 %while.1 = (s32[]{:T(128)}, f32[896,896]{0,1:T(8,128)}, s32[7,2]{0,1:T(2,128)S(1)}, f32[7,128,128]{2,1,0:T(8,128)}, s32[]{:T(128)}) while((s32[]{:T(128)}, f32[896,896]{0,1:T(8,128)}, s32[7,2]{0,1:T(2,128)S(1)}, f32[7,128,128]{2,1,0:T(8,128)}, s32[]{:T(128)}) %tuple.49), condition=%wide.while_cond, body=%wide.while_body.sunk | while | flops 2 | bytes 393329 | solution.py:38
  508.6 70.2 %custom-call.60 = f32[7,128,128]{1,2,0:T(8,128)} custom-call(f32[7,128,128]{2,1,0:T(8,128)} %get-tuple-element.10), custom_call_target="InvertDiagBlocksLowerTriangular" | custom-call | tf_op jit(solution)/shard_map/triangular_solve | solution.py:38
  599.6 149.7 %fusion = f32[32,896]{1,0:T(8,128)S(1)} fusion(f32[1792,896]{1,0:T(8,128)} %fusion.65), kind=kCustom, calls=%all-reduce-scatter | all-reduce-scatter fusion | flops 1835009 | bytes 6538240
  757.1 17.1 %collective-permute-start.2 = (f32[32,896]{1,0:T(8,128)S(1)}, f32[32,896]{1,0:T(8,128)}, u32[]{:S(2)}, u32[]{:S(2)}) collective-permute-start(f32[32,896]{1,0:T(8,128)S(1)} %fusion), channel_id=1, source_target_pairs={{0,12},{4,16},{8,20},{12,24},{16,28},{20,32},{24,36},{28,40},{32,4... | collective-permute-start | bytes 344072
  780.1 14.1 %concatenate.22 = f32[284,896]{1,0:T(8,128)} concatenate(f32[28,896]{1,0:T(8,128)} %copy-done.14, f32[32,896]{1,0:T(8,128)S(1)} %collective-permute-done.6, f32[32,896]{1,0:T(8,128)S(1)} %collective-permute-done.5, f32[32,896]{1,0:T(8,128)} %collective-permute-done.4, f32[32,896]{1,0:T(8,128)} %collective-permute-done.3, f32[32,896]{1,0:T(8,128)} %collective-permute-done.2, ...), dimensions={0} | concatenate | bytes 2035712
  795.1 78.0 %psum.23 = f32[896]{0:T(1024)S(1)} all-reduce(f32[896]{0:T(1024)S(1)} %multiply_reduce_fusion), channel_id=1, replica_groups=mesh['fsdp'=64,'tp'=4] {'fsdp','tp'}, use_global_device_ids=true, to_apply=%region_18.19 | all-reduce | flops 896 | bytes 7168 | tf_op jit(solution)/shard_map/psum | solution.py:61
  876.8 74.5 %all-gather.3.cloned.1.call-done = bf16[64,28,896]{2,1,0:T(8,128)(2,1)} async-done(((bf16[1,28,896]{2,1,0:T(8,128)(2,1)}), bf16[64,28,896]{2,1,0:T(8,128)(2,1)}) %all-gather.3.cloned.1.call-update) | async-done | bytes 3211280 | tf_op jit(solution)/shard_map/all_gather | solution.py:64
  951.2 6.0 reshape.89
  (166 shorter events, 139.1 us)
Async XLA Ops:
  7.2 1.9 copy-start
  7.2 59.4 %all-reduce.6.cloned.1.call-start = ((), (), s32[]{:S(2)}) async-start(), calls=%async_computation | async-start | bytes 2064384 | tf_op jit(solution)/shard_map/psum | solution.py:48
  13.1 256.0 %all-reduce.8.cloned.1.call-start = ((), (), s32[]{:S(2)}) async-start(), calls=%async_computation.1 | async-start | bytes 6422528 | tf_op jit(solution)/shard_map/psum | solution.py:49
  75.5 875.8 %all-gather.3.cloned.1.call-start = ((), (), s32[]{:S(2)}) async-start(), calls=%async_computation.2 | async-start | bytes 3727360 | tf_op jit(solution)/shard_map/all_gather | solution.py:64
  280.7 1.7 copy-start.5
  332.7 1.0 copy-start.12
  332.8 1.1 copy-start.11
  334.4 1.7 copy-start.1
  478.6 3.8 copy-start.15
  578.9 6.2 copy-start.4
  578.9 7.6 copy-start.13
  588.4 6.5 copy-start.2
  588.4 6.4 copy-start.6
  749.3 24.9 %collective-permute-start.6 = (f32[32,896]{1,0:T(8,128)S(1)}, f32[32,896]{1,0:T(8,128)S(1)}, u32[]{:S(2)}, u32[]{:S(2)}) collective-permute-start(f32[32,896]{1,0:T(8,128)S(1)} %fusion), channel_id=1, source_target_pairs={{0,28},{4,32},{8,36},{12,40},{16,44},{20,48},{24,52},{28,56},{32,6... | collective-permute-start | bytes 344072
  750.6 25.6 %collective-permute-start.5 = (f32[32,896]{1,0:T(8,128)S(1)}, f32[32,896]{1,0:T(8,128)S(1)}, u32[]{:S(2)}, u32[]{:S(2)}) collective-permute-start(f32[32,896]{1,0:T(8,128)S(1)} %fusion), channel_id=1, source_target_pairs={{0,24},{4,28},{8,32},{12,36},{16,40},{20,44},{24,48},{28,52},{32,5... | collective-permute-start | bytes 344072
  751.9 5.2 collective-permute-start.7
  753.2 26.8 %collective-permute-start.4 = (f32[32,896]{1,0:T(8,128)S(1)}, f32[32,896]{1,0:T(8,128)}, u32[]{:S(2)}, u32[]{:S(2)}) collective-permute-start(f32[32,896]{1,0:T(8,128)S(1)} %fusion), channel_id=1, source_target_pairs={{0,20},{4,24},{8,28},{12,32},{16,36},{20,40},{24,44},{28,48},{32,5... | collective-permute-start | bytes 344072
  755.2 24.9 %collective-permute-start.3 = (f32[32,896]{1,0:T(8,128)S(1)}, f32[32,896]{1,0:T(8,128)}, u32[]{:S(2)}, u32[]{:S(2)}) collective-permute-start(f32[32,896]{1,0:T(8,128)S(1)} %fusion), channel_id=1, source_target_pairs={{0,16},{4,20},{8,24},{12,28},{16,32},{20,36},{24,40},{28,44},{32,4... | collective-permute-start | bytes 344072
  757.1 19.1 %copy-start.14 = (f32[28,896]{1,0:T(8,128)}, f32[28,896]{1,0:T(8,128)S(1)}, u32[]{:S(2)}) copy-start(f32[28,896]{1,0:T(8,128)S(1)} %collective-permute-done.7) | copy-start | bytes 301060
  757.1 22.9 %collective-permute-start.2 = (f32[32,896]{1,0:T(8,128)S(1)}, f32[32,896]{1,0:T(8,128)}, u32[]{:S(2)}, u32[]{:S(2)}) collective-permute-start(f32[32,896]{1,0:T(8,128)S(1)} %fusion), channel_id=1, source_target_pairs={{0,12},{4,16},{8,20},{12,24},{16,28},{20,32},{24,36},{28,40},{32,4... | collective-permute-start | bytes 344072
  774.3 5.8 collective-permute-start.1
  776.2 3.9 collective-permute-start
  957.2 4.7 copy-start.3
  957.2 4.7 copy-start.7
  (3 other events, 2.5 us)
Sparse Core Ops, SparseCore 0:
  13.3 53.2 all-reduce.5
  75.6 193.4 all-reduce.7
  874.8 76.3 all-gather.2
where the time goes:
time: 979 us; the launch traced here: 971 us
  waiting for transfers between devices  321 us (33%)
  other arithmetic  246 us (25%)
  blocking collectives  228 us (23%)
  local copies, waits for them, and re-layouts  70.4 us (7%)
  matrix products  57.7 us (6%)
  starting transfers between devices  28.8 us (3%)
  between operations  19.4 us (2%)
    psum x1, waiting for transfers between devices, body(): summed = lax.psum(gram_payload(projected), 'fsdp')  193 us
    another operation x26, other arithmetic, body(): lower_factor = jnp.linalg.cholesky(gram_matrix(summed, rank_size))  157 us
    unnamed x1, blocking collectives  150 us
    psum x1, blocking collectives, body(): lax.psum(jnp.sum(right_factor * right_factor, axis=0), ('fsdp', 'tp'))  78 us
    another operation x3, other arithmetic, solve_rows(): lax.linalg.triangular_solve(lower_factor, rows_in, left_side=False, lower...  74.6 us
    all_gather x1, waiting for transfers between devices, body(): new_basis = lax.all_gather(basis_piece, 'fsdp', axis=0, tiled=True)  74.5 us
    psum x1, waiting for transfers between devices, body(): projected = lax.psum(partial_proj, 'tp')  53.4 us
    unnamed x36, local copies, waits for them, and re-layouts  29.9 us
  transfers between devices with their start and end apart: 11, of which 3 were waited for; matrix products, arithmetic and copies ran while one was open for 0% of the time, Pallas kernels for 0%

commit v1 on v0

v1 whole, which is shorter than its diff:
```python
import math

import jax
import jax.numpy as jnp
from jax import lax
from jax.experimental import pallas as pl
from jax.experimental.pallas import tpu as pltpu
from jax.sharding import PartitionSpec as P

ROWS_FF = 18432
COLS_D = 7168
RANK = 896

RIDGE = 0.001
DECAY = 0.8
EPS = 1e-06
HI = lax.Precision.HIGHEST
F32 = jnp.float32
BF16 = jnp.bfloat16
NB = 128
NBLK = RANK // NB
MESH = pl.DeviceIdType.MESH
NX, NY, NZ = 4, 4, 8


class Links:
    def __init__(self):
        f = lax.axis_index("fsdp")
        self.x = lax.axis_index("tp")
        self.core = lax.rem(f, 2)
        self.z = lax.rem(f // 2, NZ)
        self.y = f // (2 * NZ)

    def at_x(self, d):
        t = lax.rem(self.x + d, NX)
        return t, {"tp": t}

    def at_y(self, d):
        t = lax.rem(self.y + d, NY)
        return t, {"fsdp": (t * NZ + self.z) * 2 + self.core}

    def at_z(self, d):
        t = lax.rem(self.z + d, NZ)
        return t, {"fsdp": (self.y * NZ + t) * 2 + self.core}

    def at_zc(self, d):
        t = lax.rem(self.z * 2 + self.core + d, 2 * NZ)
        return t, {"fsdp": self.y * NZ * 2 + t}

    def at_xy(self, dx, dy):
        tx, ty = lax.rem(self.x + dx, NX), lax.rem(self.y + dy, NY)
        return tx * NY + ty, {"tp": tx, "fsdp": (ty * NZ + self.z) * 2 + self.core}

    def at_core(self):
        t = 1 - self.core
        return t, {"fsdp": (self.y * NZ + self.z) * 2 + t}


class Copies:
    def __init__(self, send_sems, recv_sems):
        self.send_sems, self.recv_sems = send_sems, recv_sems
        self.count = 0
        self.started = []

    def start(self, src, dst, device, when=None):
        copy = pltpu.make_async_remote_copy(
            src_ref=src, dst_ref=dst, send_sem=self.send_sems.at[self.count],
            recv_sem=self.recv_sems.at[self.count], device_id=device, device_id_type=MESH)
        self.count += 1
        if when is None:
            copy.start()
        else:
            pl.when(when)(copy.start)
        self.started.append((copy, when))
        return copy

    def finish(self):
        for copy, when in self.started:
            if when is None:
                copy.wait_send()
            else:
                pl.when(when)(copy.wait_send)
        self.started = []


def greet(links, along):
    barrier = pltpu.get_barrier_semaphore()
    partners = []
    if "x" in along:
        partners += [links.at_x(d)[1] for d in range(1, NX)]
    if "y" in along:
        partners += [links.at_y(d)[1] for d in range(1, NY)]
    if "z" in along:
        partners += [links.at_z(d)[1] for d in range(1, NZ)]
    if "c" in along:
        partners += [links.at_core()[1]]
    if "Z" in along:
        partners += [links.at_zc(d)[1] for d in range(1, 2 * NZ)]
    if "X" in along:
        partners += [links.at_xy(dx, dy)[1] for dx in range(NX) for dy in range(NY) if dx or dy]
    for device in partners:
        pl.semaphore_signal(barrier, inc=1, device_id=device, device_id_type=MESH)
    return barrier, len(partners)


def rows(start, size):
    return pl.ds(pl.multiple_of(start, 8), size)


GRAM_COPIES = 3 + 1 + 6 + 6 + 7 + 3 + 6 + 6 + 1 + 1


def cross_half(low, projected, half):
    lhs = low[:, pl.ds(pl.multiple_of(half * RANK, NB), RANK)]
    p = projected[...]
    high = p.astype(BF16)
    rest = (p - high.astype(F32)).astype(BF16)
    dims = (((0,), (0,)), ((), ()))
    return (lax.dot_general(lhs, high, dims, preferred_element_type=F32)
            + lax.dot_general(lhs, rest, dims, preferred_element_type=F32))


def gram_kernel(mom, grad, basis, p_out, g_out, s_out, pp, prx, pc, pf, ga, r1, s1, r2, zr, a4, gf, low, so, sr, ssem, rsem):
    lk = Links()
    cp = Copies(ssem, rsem)
    barrier, partners = greet(lk, "xyzc")
    part = pp.shape[0] // NX
    step = 96
    for c in range(pp.shape[0] // step):
        at = pl.ds(c * step, step)
        low[at, :] = (mom[at, :] + grad[at, :].astype(F32)).astype(BF16)
        pp[at, :] = jnp.dot(low[at, :], basis[...], preferred_element_type=F32)
    pl.semaphore_wait(barrier, partners)
    sent = []
    for d in range(1, NX):
        t, dev = lk.at_x(d)
        sent.append(cp.start(pp.at[rows(t * part, part)], prx.at[d - 1], dev))
    for copy in sent:
        copy.wait_recv()
    mine = pp[rows(lk.x * part, part), :] + prx[0] + prx[1] + prx[2]
    pf[rows(lk.x * part, part), :] = mine
    pc[rows(lk.core * part, part), pl.ds(0, RANK)] = mine
    half = pc.at[rows(lk.core * part, part), pl.ds(0, RANK)]
    copy = cp.start(half, half, lk.at_core()[1])
    copy.wait_recv()
    pc[:, pl.ds(RANK, 3 * NB)] = pc[:, pl.ds(0, 3 * NB)]
    for b in range(NBLK):
        blocks = lax.dot_general(
            pc[:, pl.ds(b * NB, NB)],
            pc[:, pl.ds(pl.multiple_of((b + 2 * lk.core) * NB, NB), 2 * NB)],
            (((0,), (0,)), ((), ())), precision=HI, preferred_element_type=F32)
        ga[0, pl.ds(b * NB, NB), :] = blocks[:, :NB]
        ga[1, pl.ds(b * NB, NB), :] = blocks[:, NB:]
    big, small = RANK // 4, RANK // 16
    sent = []
    for d in range(1, 4):
        tx, dx = lk.at_x(d)
        ty, dy = lk.at_y(d)
        sent.append(cp.start(ga.at[0, rows(tx * big, big)], r1.at[0, d - 1], dx))
        sent.append(cp.start(ga.at[1, rows(ty * big, big)], r1.at[1, d - 1], dy))
    for copy in sent:
        copy.wait_recv()
    s1[0] = ga[0, rows(lk.x * big, big), :] + r1[0, 0] + r1[0, 1] + r1[0, 2]
    s1[1] = ga[1, rows(lk.y * big, big), :] + r1[1, 0] + r1[1, 1] + r1[1, 2]
    sent = []
    for d in range(1, 4):
        tx, dx = lk.at_x(d)
        ty, dy = lk.at_y(d)
        sent.append(cp.start(s1.at[0, rows(ty * small, small)], r2.at[0, d - 1], dy))
        sent.append(cp.start(s1.at[1, rows(tx * small, small)], r2.at[1, d - 1], dx))
    for copy in sent:
        copy.wait_recv()
    zr[lk.z, pl.ds(0, small), :] = s1[0, rows(lk.y * small, small), :] + r2[0, 0] + r2[0, 1] + r2[0, 2]
    zr[lk.z, pl.ds(small, small), :] = s1[1, rows(lk.x * small, small), :] + r2[1, 0] + r2[1, 1] + r2[1, 2]
    sent = []
    for d in range(1, NZ):
        sent.append(cp.start(zr.at[lk.z], zr.at[lk.z], lk.at_z(d)[1]))
    rest = []
    own_rows = pf.at[rows(lk.x * part, part)]
    for d in range(1, NX):
        rest.append(cp.start(own_rows, own_rows, lk.at_x(d)[1]))
    for copy in sent:
        copy.wait_recv()
    total = zr[0]
    for i in range(1, NZ):
        total = total + zr[i]
    a4[0, rows(lk.y * small, small), :] = total[:small]
    a4[1, rows(lk.x * small, small), :] = total[small:]
    sent = []
    for d in range(1, 4):
        own0 = a4.at[0, rows(lk.y * small, small)]
        own1 = a4.at[1, rows(lk.x * small, small)]
        sent.append(cp.start(own0, own0, lk.at_y(d)[1]))
        sent.append(cp.start(own1, own1, lk.at_x(d)[1]))
    for copy in rest:
        copy.wait_recv()
    so[...] = cross_half(low, pf, 1 - lk.core)
    cross = cp.start(so, sr, lk.at_core()[1])
    for copy in sent:
        copy.wait_recv()
    gf[lk.core, 0, rows(lk.x * big, big), :] = a4[0]
    gf[lk.core, 1, rows(lk.y * big, big), :] = a4[1]
    sent = []
    for d in range(1, 4):
        own0 = gf.at[lk.core, 0, rows(lk.x * big, big)]
        own1 = gf.at[lk.core, 1, rows(lk.y * big, big)]
        sent.append(cp.start(own0, own0, lk.at_x(d)[1]))
        sent.append(cp.start(own1, own1, lk.at_y(d)[1]))
    s_out[...] = cross_half(low, pf, lk.core)
    for copy in sent:
        copy.wait_recv()
    copy = cp.start(gf.at[lk.core], gf.at[lk.core], lk.at_core()[1])
    cross.wait_recv()
    s_out[...] += sr[...]
    copy.wait_recv()
    cp.finish()
    p_out[...] = pf[...]
    g_out[...] = gf[...]


def project_and_gram(momentum, gradient, basis):
    n, big, small = momentum.shape[0], RANK // 4, RANK // 16
    vm = pl.BlockSpec(memory_space=pltpu.VMEM)
    return pl.pallas_call(
        gram_kernel,
        out_shape=(jax.ShapeDtypeStruct((n, RANK), F32), jax.ShapeDtypeStruct((2, 2, RANK, NB), F32),
                   jax.ShapeDtypeStruct((RANK, RANK), F32)),
        in_specs=[vm] * 3,
        out_specs=(vm,) * 3,
        scratch_shapes=[
            pltpu.VMEM((n, RANK), F32),
            pltpu.VMEM((3, n // NX, RANK), F32),
            pltpu.VMEM((2 * n // NX, RANK + 3 * NB), F32),
            pltpu.VMEM((n, RANK), F32),
            pltpu.VMEM((2, RANK, NB), F32),
            pltpu.VMEM((2, 3, big, NB), F32),
            pltpu.VMEM((2, big, NB), F32),
            pltpu.VMEM((2, 3, small, NB), F32),
            pltpu.VMEM((NZ, 2 * small, NB), F32),
            pltpu.VMEM((2, big, NB), F32),
            pltpu.VMEM((2, 2, RANK, NB), F32),
            pltpu.VMEM(momentum.shape, BF16),
            pltpu.VMEM((RANK, RANK), F32),
            pltpu.VMEM((RANK, RANK), F32),
            pltpu.SemaphoreType.DMA((GRAM_COPIES,)),
            pltpu.SemaphoreType.DMA((GRAM_COPIES,)),
        ],
        compiler_params=pltpu.CompilerParams(
            collective_id=0, has_side_effects=True, vmem_limit_bytes=48 * 2**20),
    )(momentum, gradient, basis)


def factor128(T):
    lane = lax.broadcasted_iota(jnp.int32, (8, 128), 1)
    sub = lax.broadcasted_iota(jnp.int32, (8, 128), 0)
    T = list(T)
    out = []
    for s in range(16):
        V = T[s]
        def lb(x, c):
            return jnp.broadcast_to(x[:, c:c + 1], (8, 128))
        def sb(x, r):
            return jnp.broadcast_to(x[r:r + 1, :], (8, 128))
        E = [lb(V, 8 * s + c) for c in range(8)]
        a = {}
        for c in range(8):
            for r in range(c, 8):
                a[r, c] = sb(E[c], r)
        inblk = (lane >= 8 * s) & (lane < 8 * s + 8)
        Vp = jnp.where(inblk, jnp.where(lane - 8 * s == sub, 1.0, 0.0), V)
        y = [sb(Vp, r) for r in range(8)]
        rp = [None] * 8
        d = [None] * 8
        l = {}
        for j in range(8):
            d[j] = a[j, j]
            rp[j] = pl.reciprocal(d[j], approx=False)
            for i in range(j + 1, 8):
                l[i, j] = a[i, j] * rp[j]
            for i in range(j + 1, 8):
                for k in range(j + 1, i + 1):
                    a[i, k] = a[i, k] - l[i, j] * a[k, j]
            for i in range(j + 1, 8):
                y[i] = y[i] - l[i, j] * y[j]
        z = [y[j] * rp[j] for j in range(8)]
        R = y[0] * lax.rsqrt(d[0])
        for j in range(1, 8):
            R = jnp.where(sub == j, y[j] * lax.rsqrt(d[j]), R)
        out.append(jnp.where(lane < 8 * s + 8, R, 0.0))
        if s < 15:
            q = [None] * 8
            for j in range(7, -1, -1):
                acc = z[j]
                for i in range(j + 1, 8):
                    acc = acc - l[i, j] * q[i]
                q[j] = acc
            for t in range(s + 1, 16):
                Et = [lb(T[t], 8 * s + c) for c in range(8)]
                base = jnp.where(inblk, 0.0, T[t])
                if t == s + 1:
                    for j in range(8):
                        for i in range(j + 1, 8):
                            Et[i] = Et[i] - l[i, j] * Et[j]
                    acc = base
                    for j in range(8):
                        acc = acc - Et[j] * z[j]
                else:
                    acc = base
                    for j in range(8):
                        acc = acc - Et[j] * q[j]
                T[t] = acc
    return out


def assemble(g_ref, w):
    eye = jnp.where(
        lax.broadcasted_iota(jnp.int32, (NB, NB), 0) == lax.broadcasted_iota(jnp.int32, (NB, NB), 1), RIDGE, 0.0)
    for d in range(4):
        for b in range(NBLK):
            c = (b + d) % NBLK
            block = g_ref[d // 2, d % 2, b * NB:(b + 1) * NB, :]
            if d == 0:
                block = block + eye
            if b <= c:
                w[b * NB:(b + 1) * NB, c * NB:(c + 1) * NB] = block
            else:
                w[c * NB:(c + 1) * NB, b * NB:(b + 1) * NB] = block.T


def factor_step(w, k):
    o = pl.multiple_of(k * NB, NB)
    tiles = [w[pl.ds(pl.multiple_of(o + 8 * t, 8), 8), pl.ds(o, NB)] for t in range(16)]
    diag = jnp.concatenate(factor128(tiles), axis=0)
    w[pl.ds(o, NB), :] = jnp.dot(diag, w[pl.ds(o, NB), :], precision=HI, preferred_element_type=F32)
    w[pl.ds(o, NB), pl.ds(o, NB)] = diag

    def update(i, _):
        r = pl.multiple_of(i * NB, NB)
        upper = w[pl.ds(o, NB), pl.ds(r, NB)]
        w[pl.ds(r, NB), pl.ds(o, NB)] = jnp.zeros((NB, NB), F32)
        w[pl.ds(r, NB), :] -= lax.dot_general(
            upper, w[pl.ds(o, NB), :], (((0,), (0,)), ((), ())), precision=HI, preferred_element_type=F32)
        return 0

    lax.fori_loop(k + 1, NBLK, update, 0)


def times_inverse(left, w, k):
    n = (k + 1) * NB
    return lax.dot_general(
        left[:, :n], w[k * NB:n, :n], (((1,), (1,)), ((), ())), precision=HI, preferred_element_type=F32)


OWN = 7
FACTOR_COPIES = 3 + 7 + 7 + 3 + 15 + 15 + 7 + 3 + 3 + 7 + 1


def factor_kernel(g_ref, s_ref, p_ref, nb_out, low_out, w, ra1, rb1, sa, sb, ra2, rb2, rf, sq1, sq2, nb, ssem, rsem):
    lk = Links()
    cp = Copies(ssem, rsem)
    barrier, partners = greet(lk, "ZX")
    owner = lk.z < OWN
    zc = jnp.minimum(lk.z, OWN - 1)
    assemble(g_ref, w)
    pl.semaphore_wait(barrier, partners)
    half = RANK // 2
    ya, za, piece = half // NY, half // OWN, half // NY // OWN
    first_a, first_b = [], []
    for d in range(1, NY):
        t, dev = lk.at_y(d)
        first_a.append(cp.start(s_ref.at[rows(t * ya, ya)], ra1.at[d - 1], dev))
    for d in range(1, NZ):
        t, dev = lk.at_z(d)
        src = s_ref.at[rows(half + jnp.minimum(t, OWN - 1) * za, za)]
        first_b.append(cp.start(src, rb1.at[d - 1], dev, when=t < OWN))
    lax.fori_loop(0, 3, lambda k, _: (factor_step(w, k), 0)[1], 0)
    for copy in first_a:
        copy.wait_recv()
    sa[...] = s_ref[rows(lk.y * ya, ya), :] + ra1[0] + ra1[1] + ra1[2]
    second_a, second_b = [], []
    for d in range(1, NZ):
        t, dev = lk.at_z(d)
        src = sa.at[rows(jnp.minimum(t, OWN - 1) * piece, piece)]
        second_a.append(cp.start(src, ra2.at[d - 1], dev, when=t < OWN))
    lax.fori_loop(3, 6, lambda k, _: (factor_step(w, k), 0)[1], 0)

    @pl.when(owner)
    def _():
        for copy in first_b:
            copy.wait_recv()
        total = s_ref[rows(half + zc * za, za), :]
        for i in range(OWN):
            total = total + rb1[i]
        sb[...] = total

    for d in range(1, NY):
        t, dev = lk.at_y(d)
        second_b.append(cp.start(sb.at[rows(t * piece, piece)], rb2.at[d - 1], dev, when=owner))
    lax.fori_loop(6, NBLK, lambda k, _: (factor_step(w, k), 0)[1], 0)

    @pl.when(owner)
    def _():
        for copy in second_a:
            copy.wait_recv()
        total = sa[rows(zc * piece, piece), :]
        for i in range(OWN):
            total = total + ra2[i]
        rf[0:piece, :] = total
        for copy in second_b:
            copy.wait_recv()
        rf[piece:2 * piece, :] = sb[rows(lk.y * piece, piece), :] + rb2[0] + rb2[1] + rb2[2]

    @pl.when(jnp.logical_not(owner))
    def _():
        rf[...] = jnp.zeros_like(rf)

    left = rf[...]
    right = [times_inverse(left, w, k) for k in range(NBLK)]
    me1 = lk.z * 2 + lk.core
    me2 = lk.x * NY + lk.y
    for k in range(NBLK):
        sq1[me1, k:k + 1, :] = jnp.sum(right[k] * right[k], axis=0, keepdims=True)
    sq1[me1, NBLK:, :] = jnp.zeros((1, NB), F32)
    sent = [cp.start(sq1.at[me1], sq1.at[me1], lk.at_zc(d)[1]) for d in range(1, 2 * NZ)]
    for copy in sent:
        copy.wait_recv()
    total = sq1[0]
    for i in range(1, 2 * NZ):
        total = total + sq1[i]
    sq2[me2] = total
    sent = [cp.start(sq2.at[me2], sq2.at[me2], lk.at_xy(dx, dy)[1])
            for dx in range(NX) for dy in range(NY) if dx or dy]
    for copy in sent:
        copy.wait_recv()
    total = sq2[0]
    for i in range(1, NX * NY):
        total = total + sq2[i]
    rms = jnp.sqrt(total / COLS_D + EPS)
    base = lk.core * RANK
    for k in range(NBLK):
        at = slice(k * NB, (k + 1) * NB)
        normal = (right[k] / rms[k:k + 1, :]).astype(BF16)

        @pl.when(owner)
        def _():
            nb[rows16(base + lk.y * ya + zc * piece, piece), at] = normal[:piece]
            nb[rows16(base + half + zc * za + lk.y * piece, piece), at] = normal[piece:]

    ga, gb = [], []
    own_a = nb.at[rows16(base + lk.y * ya + zc * piece, piece)]
    own_b = nb.at[rows16(base + half + zc * za + lk.y * piece, piece)]
    for d in range(1, NY):
        gb.append(cp.start(own_b, own_b, lk.at_y(d)[1], when=owner))
    for d in range(1, NZ):
        ga.append(cp.start(own_a, own_a, lk.at_z(d)[1], when=owner))

    @pl.when(owner)
    def _():
        for copy in gb:
            copy.wait_recv()

    gb = []
    own_b = nb.at[rows16(base + half + zc * za, za)]
    for d in range(1, NZ):
        gb.append(cp.start(own_b, own_b, lk.at_z(d)[1], when=owner))
    for d in range(1, NZ):
        pl.when(lax.rem(lk.z + NZ - d, NZ) < OWN)(ga[d - 1].wait_recv)
    ga = []
    own_a = nb.at[rows16(base + lk.y * ya, ya)]
    for d in range(1, NY):
        ga.append(cp.start(own_a, own_a, lk.at_y(d)[1]))
    left = p_ref[...]
    n = p_ref.shape[0]
    for k in range(NBLK):
        at = slice(k * NB, (k + 1) * NB)
        ortho = times_inverse(left, w, k)
        low_out[:n, at] = (ortho * rms[k:k + 1, :]).astype(BF16)
        low_out[n:, at] = ortho.astype(BF16)
    for copy in ga:
        copy.wait_recv()
    for d in range(1, NZ):
        pl.when(lax.rem(lk.z + NZ - d, NZ) < OWN)(gb[d - 1].wait_recv)
    own = nb.at[rows16(base, RANK)]
    copy = cp.start(own, own, lk.at_core()[1])
    copy.wait_recv()
    cp.finish()
    nb_out[...] = nb[...]


def rows16(start, size):
    return pl.ds(pl.multiple_of(start, 16), size)


def factor_and_basis(gram, cross, projected):
    n = projected.shape[0]
    vm = pl.BlockSpec(memory_space=pltpu.VMEM)
    half = RANK // 2
    ya, za, piece = half // NY, half // OWN, half // NY // OWN
    return pl.pallas_call(
        factor_kernel,
        out_shape=(jax.ShapeDtypeStruct((2 * RANK, RANK), BF16), jax.ShapeDtypeStruct((2 * n, RANK), BF16)),
        in_specs=[vm] * 3,
        out_specs=(vm, vm),
        scratch_shapes=[
            pltpu.VMEM((RANK, RANK), F32),
            pltpu.VMEM((NY - 1, ya, RANK), F32),
            pltpu.VMEM((NZ - 1, za, RANK), F32),
            pltpu.VMEM((ya, RANK), F32),
            pltpu.VMEM((za, RANK), F32),
            pltpu.VMEM((NZ - 1, piece, RANK), F32),
            pltpu.VMEM((NY - 1, piece, RANK), F32),
            pltpu.VMEM((2 * piece, RANK), F32),
            pltpu.VMEM((2 * NZ, 8, NB), F32),
            pltpu.VMEM((NX * NY, 8, NB), F32),
            pltpu.VMEM((2 * RANK, RANK), BF16),
            pltpu.SemaphoreType.DMA((FACTOR_COPIES,)),
            pltpu.SemaphoreType.DMA((FACTOR_COPIES,)),
        ],
        compiler_params=pltpu.CompilerParams(
            collective_id=1, has_side_effects=True, vmem_limit_bytes=48 * 2**20),
    )(gram, cross, projected)


def body(momentum, gradient, column_basis):
    projected, gram, cross = project_and_gram(momentum, gradient, column_basis)
    new_basis, stacked = factor_and_basis(gram, cross, projected)
    blended = momentum + gradient.astype(F32)
    products = lax.dot_general(
        stacked, new_basis, (((1,), (1,)), ((), ())), preferred_element_type=F32
    )
    rows_here = momentum.shape[0]
    momentum_new = blended - (1.0 - DECAY) * products[:rows_here]
    update = (math.sqrt(ROWS_FF / RANK) * products[rows_here:]).astype(BF16)
    return (momentum_new, update, new_basis)


def solution(mesh):
    placed = (P("fsdp", "tp"), P("fsdp", "tp"), P("tp", None))
    return jax.shard_map(
        body,
        mesh=mesh,
        in_specs=placed,
        out_specs=(P("fsdp", "tp"), P("fsdp", "tp"), P("tp", None)),
        check_vma=False,
    )
```

time: 979 us -> 183 us (0.19)
  waiting for transfers between devices: 321 us -> 0 us
  other arithmetic: 246 us -> 2.11 us
  blocking collectives: 228 us -> 0 us
  Pallas kernels: 0 us -> 170 us
  local copies, waits for them, and re-layouts: 70.4 us -> 5.4 us
  matrix products: 57.7 us -> 4.39 us
  starting transfers between devices: 28.8 us -> 0 us
  between operations: 19.4 us -> 0.7 us
    psum x2 -> x0, waiting for transfers between devices: 246 us -> none  [the longest x1 193 us: body(): summed = lax.psum(gram_payload(projected), 'fsdp')]
    another operation x29 -> x0, other arithmetic: 232 us -> none  [the longest x26 157 us: body(): lower_factor = jnp.linalg.cholesky(gram_matrix(summed, rank_size))]
    pallas_call x0 -> x2, Pallas kernels: none -> 170 us  [the longest x1 103 us: factor_and_basis(): pl.pallas_call(factor_kernel, out_shape=(jax.ShapeDtypeStruct((2 * RANK,...]
    unnamed x1 -> x0, blocking collectives: 150 us -> none
    psum x1 -> x0, blocking collectives: 78 us -> none  [body(): lax.psum(jnp.sum(right_factor * right_factor, axis=0), ('fsdp', 'tp'))]
    all_gather x1 -> x0, waiting for transfers between devices: 74.5 us -> none  [body(): new_basis = lax.all_gather(basis_piece, 'fsdp', axis=0, tiled=True)]
    another operation x58 -> x0, local copies, waits for them, and re-layouts: 35.9 us -> none
    another operation x25 -> x0, matrix products: 35.4 us -> none  [the longest x12 21.4 us: body(): lower_factor = jnp.linalg.cholesky(gram_matrix(summed, rank_size))]
  transfers between devices with their start and end apart: 11 -> 0, of which waited for: 3 -> 0; matrix products, arithmetic and copies ran while one was open for 0% -> 0% of each run, Pallas kernels for 0% -> 0%
where the time goes in v1:
time: 183 us; the launch traced here: 182 us
  Pallas kernels  170 us (93%)
  local copies, waits for them, and re-layouts  5.4 us (3%)
  matrix products  4.39 us (2%)
  other arithmetic  2.11 us (1%)
    pallas_call x1, Pallas kernels, factor_and_basis(): pl.pallas_call(factor_kernel, out_shape=(jax.ShapeDtypeStruct((2 * RANK,...  103 us
    pallas_call x1, Pallas kernels, project_and_gram(): pl.pallas_call(gram_kernel, out_shape=(jax.ShapeDtypeStruct((n, RANK), F3...  66.7 us
    unnamed x11, local copies, waits for them, and re-layouts  5.4 us
    dot_general x1, matrix products, body(): lax.dot_general(stacked, new_basis, (((1,), (1,)), ((), ())), preferred_e...  4.39 us

profile of v1, /device:TPU:1, one launch (start us, length us, event | category | flops | bytes accessed | tf_op | source)
XLA Modules:
  0.0 182.5 jit_solution(8807356961770857732)
XLA Ops:
  0.6 0.0 copy-start
  0.6 1.6 copy-done
  2.2 0.0 copy-start.2
  2.2 1.2 copy-done.2
  3.4 66.7 %shard_map.58 = (f32[288,896]{1,0:T(8,128)S(1)}, f32[2,2,896,128]{3,2,1,0:T(8,128)S(1)}, f32[896,896]{1,0:T(8,128)}) custom-call(f32[288,1792]{1,0:T(8,128)S(1)} %copy-done, bf16[288,1792]{1,0:T(8,128)(2,1)S(1)} %copy-done.2, bf16[1792,896]{1,0:T(8,128)(2,1)} %basis.1), custom_call_target="tpu_custom_call" | custom-call | tf_op jit(solution)/shard_map/pallas_call | solution.py:224
  70.2 103.1 %shard_map.59 = (bf16[1792,896]{1,0:T(8,128)(2,1)}, bf16[576,896]{1,0:T(8,128)(2,1)S(1)}) custom-call(f32[2,2,896,128]{3,2,1,0:T(8,128)S(1)} %get-tuple-element.8.g_ref, f32[896,896]{1,0:T(8,128)} %get-tuple-element.9.s_ref, f32[288,896]{1,0:T(8,128)S(1)} %get-tuple-element.10.p_ref), custom_call_target="tpu_custom_call" | custom-call | tf_op jit(solution)/shard_map/pallas_call | solution.py:499
  173.3 0.0 copy-start.1
  173.3 0.0 copy-start.3
  173.3 4.4 %fusion.2 = f32[576,1792]{1,0:T(8,128)S(1)} fusion(bf16[576,896]{1,0:T(8,128)(2,1)S(1)} %get-tuple-element.11, bf16[1792,896]{1,0:T(8,128)(2,1)} %get-tuple-element.20), kind=kOutput, calls=%fused_computation.4 | convolution fusion | flops 1849688064 | bytes 8372224 | tf_op jit(solution)/shard_map/dot_general | solution.py:528
  177.7 0.0 copy-done.1
  177.7 0.0 copy-done.3
  177.8 0.0 copy-start.4
  177.8 2.1 %fusion = (bf16[288,1792]{1,0:T(8,128)(2,1)}, f32[288,1792]{1,0:T(8,128)}) fusion(f32[576,1792]{1,0:T(8,128)S(1)} %fusion.2, f32[288,1792]{1,0:T(8,128)S(1)} %copy-done.1, bf16[288,1792]{1,0:T(8,128)(2,1)S(1)} %copy-done.3), kind=kLoop, calls=%fused_computation.1 | loop fusion | flops 3096576 | bytes 10321920 | tf_op jit(solution)/shard_map/convert_element_type | solution.py:533
  179.9 0.9 copy-done.4
  180.8 1.7 copy.7
Async XLA Ops:
  0.6 1.6 copy-start
  2.2 1.2 copy-start.2
  173.3 4.4 %copy-start.1 = (f32[288,1792]{1,0:T(8,128)S(1)}, f32[288,1792]{1,0:T(8,128)}, u32[]{:S(2)}) copy-start(f32[288,1792]{1,0:T(8,128)} %mom.1) | copy-start | bytes 6193156
  173.3 4.4 %copy-start.3 = (bf16[288,1792]{1,0:T(8,128)(2,1)S(1)}, bf16[288,1792]{1,0:T(8,128)(2,1)}, u32[]{:S(2)}) copy-start(bf16[288,1792]{1,0:T(8,128)(2,1)} %grad.1) | copy-start | bytes 3096580
  177.8 3.0 %copy-start.4 = (bf16[1792,896]{1,0:T(8,128)(2,1)S(1)}, bf16[1792,896]{1,0:T(8,128)(2,1)}, u32[]{:S(2)}) copy-start(bf16[1792,896]{1,0:T(8,128)(2,1)} %get-tuple-element.20) | copy-start | bytes 9633796

commit v2 on v0

v2 whole, which is shorter than its diff:
```python
import math

import jax
import jax.numpy as jnp
from jax import lax
from jax.experimental import pallas as pl
from jax.experimental.pallas import tpu as pltpu
from jax.sharding import PartitionSpec as P

ROWS_FF = 18432
COLS_D = 7168
RANK = 896

RIDGE = 0.001
DECAY = 0.8
EPS = 1e-06
HI = lax.Precision.HIGHEST
F32 = jnp.float32
BF16 = jnp.bfloat16
NB = 128
NBLK = RANK // NB
MESH = pl.DeviceIdType.MESH
NX, NY, NZ = 4, 4, 8


class Links:
    def __init__(self):
        f = lax.axis_index("fsdp")
        self.x = lax.axis_index("tp")
        self.core = lax.rem(f, 2)
        self.z = lax.rem(f // 2, NZ)
        self.y = f // (2 * NZ)

    def at_x(self, d):
        t = lax.rem(self.x + d, NX)
        return t, {"tp": t}

    def at_y(self, d):
        t = lax.rem(self.y + d, NY)
        return t, {"fsdp": (t * NZ + self.z) * 2 + self.core}

    def at_z(self, d):
        t = lax.rem(self.z + d, NZ)
        return t, {"fsdp": (self.y * NZ + t) * 2 + self.core}

    def at_zc(self, d):
        t = lax.rem(self.z * 2 + self.core + d, 2 * NZ)
        return t, {"fsdp": self.y * NZ * 2 + t}

    def at_xy(self, dx, dy):
        tx, ty = lax.rem(self.x + dx, NX), lax.rem(self.y + dy, NY)
        return tx * NY + ty, {"tp": tx, "fsdp": (ty * NZ + self.z) * 2 + self.core}

    def at_core(self):
        t = 1 - self.core
        return t, {"fsdp": (self.y * NZ + self.z) * 2 + t}


class Copies:
    def __init__(self, send_sems, recv_sems):
        self.send_sems, self.recv_sems = send_sems, recv_sems
        self.count = 0
        self.started = []

    def make(self, src, dst, device, when=None, slot=None):
        arrival = self.count if slot is None else slot
        copy = pltpu.make_async_remote_copy(
            src_ref=src, dst_ref=dst, send_sem=self.send_sems.at[self.count],
            recv_sem=self.recv_sems.at[arrival], device_id=device, device_id_type=MESH)
        self.count += 1
        self.started.append((copy, when))
        return copy

    def start(self, src, dst, device, when=None, slot=None):
        copy = self.make(src, dst, device, when, slot)
        if when is None:
            copy.start()
        else:
            pl.when(when)(copy.start)
        return copy

    def finish(self):
        for copy, when in self.started:
            if when is None:
                copy.wait_send()
            else:
                pl.when(when)(copy.wait_send)
        self.started = []


def greet(links, along):
    barrier = pltpu.get_barrier_semaphore()
    partners = []
    if "x" in along:
        partners += [links.at_x(d)[1] for d in range(1, NX)]
    if "y" in along:
        partners += [links.at_y(d)[1] for d in range(1, NY)]
    if "z" in along:
        partners += [links.at_z(d)[1] for d in range(1, NZ)]
    if "c" in along:
        partners += [links.at_core()[1]]
    if "Z" in along:
        partners += [links.at_zc(d)[1] for d in range(1, 2 * NZ)]
    if "X" in along:
        partners += [links.at_xy(dx, dy)[1] for dx in range(NX) for dy in range(NY) if dx or dy]
    for device in partners:
        pl.semaphore_signal(barrier, inc=1, device_id=device, device_id_type=MESH)
    return barrier, len(partners)


def rows(start, size):
    return pl.ds(pl.multiple_of(start, 8), size)


def cross_half(low, projected, half):
    lhs = low[:, pl.ds(pl.multiple_of(half * RANK, NB), RANK)]
    p = projected[...]
    high = p.astype(BF16)
    rest = (p - high.astype(F32)).astype(BF16)
    dims = (((0,), (0,)), ((), ()))
    return (lax.dot_general(lhs, high, dims, preferred_element_type=F32)
            + lax.dot_general(lhs, rest, dims, preferred_element_type=F32))


def factor128(tiles):
    lane = lax.broadcasted_iota(jnp.int32, (8, 128), 1)
    sub = lax.broadcasted_iota(jnp.int32, (8, 128), 0)
    tiles = list(tiles)
    out = []

    def over_lanes(x, c):
        return jnp.broadcast_to(x[:, c:c + 1], (8, 128))

    def over_rows(x, r):
        return jnp.broadcast_to(x[r:r + 1, :], (8, 128))

    diag = [over_lanes(tiles[0], c) for c in range(8)]
    for s in range(16):
        a = {(r, c): over_rows(diag[c], r) for c in range(8) for r in range(c, 8)}
        inside = (lane >= 8 * s) & (lane < 8 * s + 8)
        row = jnp.where(inside, jnp.where(lane - 8 * s == sub, 1.0, 0.0), tiles[s])
        y = [over_rows(row, r) for r in range(8)]
        inv, low = [None] * 8, {}
        for j in range(8):
            inv[j] = pl.reciprocal(a[j, j], approx=False)
            for i in range(j + 1, 8):
                low[i, j] = a[i, j] * inv[j]
            for i in range(j + 1, 8):
                for k in range(j + 1, i + 1):
                    a[i, k] = a[i, k] - low[i, j] * a[k, j]
            for i in range(j + 1, 8):
                y[i] = y[i] - low[i, j] * y[j]
        z = [y[j] * inv[j] for j in range(8)]
        done = y[0] * lax.rsqrt(a[0, 0])
        for j in range(1, 8):
            done = jnp.where(sub == j, y[j] * lax.rsqrt(a[j, j]), done)
        out.append(jnp.where(lane < 8 * s + 8, done, 0.0))
        if s == 15:
            break
        q = [None] * 8
        for j in range(7, -1, -1):
            q[j] = z[j]
            for i in range(j + 1, 8):
                q[j] = q[j] - low[i, j] * q[i]
        for t in range(s + 1, 16):
            col = [over_lanes(tiles[t], 8 * s + c) for c in range(8)]
            acc = jnp.where(inside, 0.0, tiles[t])
            if t == s + 1:
                for j in range(8):
                    for i in range(j + 1, 8):
                        col[i] = col[i] - low[i, j] * col[j]
                for j in range(8):
                    acc = acc - col[j] * z[j]
                diag = [over_lanes(tiles[t], 8 * t + c) for c in range(8)]
                for j in range(8):
                    scaled = col[j] * inv[j]
                    for c in range(8):
                        diag[c] = diag[c] - col[j] * over_rows(scaled, c)
            else:
                for j in range(8):
                    acc = acc - col[j] * q[j]
            tiles[t] = acc
    return out


def assemble(g_ref, w):
    eye = jnp.where(
        lax.broadcasted_iota(jnp.int32, (NB, NB), 0) == lax.broadcasted_iota(jnp.int32, (NB, NB), 1), RIDGE, 0.0)
    for d in range(4):
        for b in range(NBLK):
            c = (b + d) % NBLK
            block = g_ref[d // 2, d % 2, b * NB:(b + 1) * NB, :]
            if d == 0:
                block = block + eye
            if b <= c:
                w[b * NB:(b + 1) * NB, c * NB:(c + 1) * NB] = block
            else:
                w[c * NB:(c + 1) * NB, b * NB:(b + 1) * NB] = block.T


def times_inverse(left, w, k):
    n = (k + 1) * NB
    return lax.dot_general(
        left[:, :n], w[k * NB:n, :n], (((1,), (1,)), ((), ())), precision=HI, preferred_element_type=F32)


def block(i):
    return slice(i * NB, (i + 1) * NB)


def dot_rows(a, b):
    return lax.dot_general(a, b, (((0,), (0,)), ((), ())), precision=HI, preferred_element_type=F32)


def split(x):
    high = x.astype(BF16)
    rest = x - high.astype(F32)
    mid = rest.astype(BF16)
    return high, mid, (rest - mid.astype(F32)).astype(BF16)


def terms(x):
    high, mid, low = split(x)
    return (high, mid, high, low, high, mid), (high, high, mid, high, low, mid)


def factor(w, lefts, rights, beside):
    w[pl.ds(RANK, NB), :] = jnp.zeros((NB, RANK), F32)
    lefts[:, pl.ds(RANK, NB)] = jnp.zeros((6 * NB, NB), BF16)

    def step(k, _):
        o = pl.multiple_of(k * NB, NB)
        at = pl.ds(o, NB)
        inv = jnp.concatenate(
            factor128([w[pl.ds(pl.multiple_of(o + 8 * t, 8), 8), at] for t in range(16)]), axis=0)
        left = jnp.concatenate(terms(inv)[0], axis=1)
        right = jnp.concatenate(terms(w[at, :])[1], axis=0)
        w[at, :] = jnp.dot(left, right, preferred_element_type=F32)
        w[at, at] = inv
        left, right = terms(w[at, :])
        for i in range(6):
            lefts[block(i), pl.ds(0, RANK)] = left[i]
            rights[block(i), :] = right[i]

        def update(i, _):
            below = pl.ds(pl.multiple_of((k + 1 + 2 * i) * NB, NB), 2 * NB)
            w[below, at] = jnp.zeros((2 * NB, NB), F32)
            w[below, :] -= lax.dot_general(
                lefts[:, below], rights[...], (((0,), (0,)), ((), ())), preferred_element_type=F32)
            return 0

        lax.fori_loop(0, (NBLK - k) // 2, update, 0)
        for when, act in beside.items():
            pl.when(k == when)(act)
        return 0

    lax.fori_loop(0, NBLK, step, 0)


OWN = 7
COPIES = 3 + 1 + 6 + 6 + 5 + 3 + 6 + 6 + 8 + 1 + 3 + 7 + 7 + 3 + 15 + 15 + 7 + 3 + 3 + 7 + 2


def step_kernel(mom_any, grad_any, basis_any, low_out, nb_out, pp, prx, pc, pf, ga, r1, s1, r2, zin, zp, zr, zt, a4, gf, low,
                so, sr, s, w, ra1, sa, ra2, ring_up, ring_down, acc_up, acc_down, sb, rb2, sq1, sq2, nb, xf,
                lefts, rights, mom, grad, basis, in_sem, ssem, rsem):
    inputs = [pltpu.make_async_copy(src, dst, in_sem.at[i])
              for i, (src, dst) in enumerate(((mom_any, mom), (grad_any, grad), (basis_any, basis)))]
    for copy in inputs:
        copy.start()
    lk = Links()
    cp = Copies(ssem, rsem)
    barrier, partners = greet(lk, "ZX")
    n = pp.shape[0]
    part = n // NX
    core_dev = lk.at_core()[1]

    def project(h):
        at = pl.ds(pl.multiple_of(h * (n // 2), 16), n // 2)
        low[at, :] = (mom[at, :] + grad[at, :].astype(F32)).astype(BF16)
        pp[at, :] = jnp.dot(low[at, :], basis[...], preferred_element_type=F32)

    for copy in inputs:
        copy.wait()
    mine_half = lk.x // 2
    project(1 - mine_half)
    pl.semaphore_wait(barrier, partners)
    sent = []
    for i in range(2):
        t = (1 - mine_half) * 2 + i
        slot = lax.rem(t - lk.x + NX, NX) - 1
        sent.append(cp.start(pp.at[rows(t * part, part)], prx.at[slot], {"tp": t}, slot=slot))
    project(mine_half)
    t = mine_half * 2 + 1 - lax.rem(lk.x, 2)
    slot = lax.rem(t - lk.x + NX, NX) - 1
    sent.append(cp.start(pp.at[rows(t * part, part)], prx.at[slot], {"tp": t}, slot=slot))
    for copy in sent:
        copy.wait_recv()
    mine = pp[rows(lk.x * part, part), :] + prx[0] + prx[1] + prx[2]
    pf[rows(lk.x * part, part), :] = mine
    pc[rows(lk.core * part, part), pl.ds(0, RANK)] = mine
    own = pc.at[rows(lk.core * part, part), pl.ds(0, RANK)]
    copy = cp.start(own, own, core_dev)
    copy.wait_recv()
    pc[:, pl.ds(RANK, 3 * NB)] = pc[:, pl.ds(0, 3 * NB)]

    for b in range(NBLK):
        blocks = dot_rows(pc[:, pl.ds(b * NB, NB)],
                          pc[:, pl.ds(pl.multiple_of((b + 2 * lk.core) * NB, NB), 2 * NB)])
        ga[0, pl.ds(b * NB, NB), :] = blocks[:, :NB]
        ga[1, pl.ds(b * NB, NB), :] = blocks[:, NB:]

    big, small = RANK // 4, RANK // 16
    sent = []
    for d in range(1, 4):
        tx, dx = lk.at_x(d)
        ty, dy = lk.at_y(d)
        sent.append(cp.start(ga.at[0, rows(tx * big, big)], r1.at[0, d - 1], dx))
        sent.append(cp.start(ga.at[1, rows(ty * big, big)], r1.at[1, d - 1], dy))
    for copy in sent:
        copy.wait_recv()
    s1[0] = ga[0, rows(lk.x * big, big), :] + r1[0, 0] + r1[0, 1] + r1[0, 2]
    s1[1] = ga[1, rows(lk.y * big, big), :] + r1[1, 0] + r1[1, 1] + r1[1, 2]
    sent = []
    for d in range(1, 4):
        tx, dx = lk.at_x(d)
        ty, dy = lk.at_y(d)
        sent.append(cp.start(s1.at[0, rows(ty * small, small)], r2.at[0, d - 1], dy))
        sent.append(cp.start(s1.at[1, rows(tx * small, small)], r2.at[1, d - 1], dx))
    rest = []
    own = pf.at[rows(lk.x * part, part)]
    for d in range(1, NX):
        rest.append(cp.start(own, own, lk.at_x(d)[1]))
    for copy in sent:
        copy.wait_recv()
    zin[0] = s1[0, rows(lk.y * small, small), :] + r2[0, 0] + r2[0, 1] + r2[0, 2]
    zin[1] = s1[1, rows(lk.x * small, small), :] + r2[1, 0] + r2[1, 1] + r2[1, 2]
    even = lax.rem(lk.z, 2)
    pair = lk.at_z(NZ + 1 - 2 * even)[1]
    copy = cp.start(zin.at[1 - even], zp, pair)
    copy.wait_recv()
    zr[lk.z // 2] = zin[even] + zp[...]
    sent = [cp.start(zr.at[lk.z // 2], zr.at[lk.z // 2], lk.at_z(d)[1]) for d in (2, 4, 6)]
    for copy in sent:
        copy.wait_recv()
    zt[even] = zr[0] + zr[1] + zr[2] + zr[3]
    copy = cp.start(zt.at[even], zt.at[even], pair)
    copy.wait_recv()

    a4[0, rows(lk.y * small, small), :] = zt[0]
    a4[1, rows(lk.x * small, small), :] = zt[1]
    sent = []
    for d in range(1, 4):
        own0 = a4.at[0, rows(lk.y * small, small)]
        own1 = a4.at[1, rows(lk.x * small, small)]
        sent.append(cp.start(own0, own0, lk.at_y(d)[1]))
        sent.append(cp.start(own1, own1, lk.at_x(d)[1]))
    for copy in sent:
        copy.wait_recv()
    gf[lk.core, 0, rows(lk.x * big, big), :] = a4[0]
    gf[lk.core, 1, rows(lk.y * big, big), :] = a4[1]
    own0 = gf.at[lk.core, 0, rows(lk.x * big, big)]
    own1 = gf.at[lk.core, 1, rows(lk.y * big, big)]
    sent = []
    for d in range(1, 4):
        sent.append((cp.start(own0, own0, lk.at_x(d)[1]), 0, lax.rem(lk.x + 4 - d, 4)))
        sent.append((cp.start(own1, own1, lk.at_y(d)[1]), 1, lax.rem(lk.y + 4 - d, 4)))
    across = [cp.start(own0, own0, core_dev), cp.start(own1, own1, core_dev)]
    for copy in rest:
        copy.wait_recv()
    so[...] = cross_half(low, pf, 1 - lk.core)
    cross = cp.start(so, sr, core_dev)
    s[...] = cross_half(low, pf, lk.core)
    for copy, h, t in sent:
        copy.wait_recv()
        piece = gf.at[lk.core, h, rows(t * big, big)]
        across.append(cp.start(piece, piece, core_dev))
    cross.wait_recv()
    s[...] += sr[...]

    half = RANK // 2
    ya, za, piece = half // NY, half // OWN, half // NY // OWN
    owner = lk.z < OWN
    zc = jnp.minimum(lk.z, OWN - 1)

    def ring_rows(shift):
        return rows(half + jnp.minimum(lax.rem(lk.z + NZ + shift, NZ), OWN - 1) * za, za)

    up, down = lk.at_z(1)[1], lk.at_z(NZ - 1)[1]
    ups = [cp.make(s.at[ring_rows(4)] if i == 0 else acc_up.at[i - 1], ring_up.at[i], up) for i in range(4)]
    downs = [cp.make(s.at[ring_rows(-3)] if i == 0 else acc_down.at[i - 1], ring_down.at[i], down) for i in range(3)]
    first_a = []
    for d in range(1, NY):
        t, dev = lk.at_y(d)
        first_a.append(cp.make(s.at[rows(t * ya, ya)], ra1.at[d - 1], dev))
    second_a = []
    for d in range(1, NZ):
        t, dev = lk.at_z(d)
        src = sa.at[rows(jnp.minimum(t, OWN - 1) * piece, piece)]
        second_a.append(cp.make(src, ra2.at[d - 1], dev))
    ring_at = {shift: ring_rows(shift) for shift in (3, 2, 1, -2, -1)}
    own_ya = rows(lk.y * ya, ya)

    def ring_step(i):
        ups[i - 1].wait_recv()
        acc_up[i - 1] = s[ring_at[4 - i], :] + ring_up[i - 1]
        ups[i].start()
        if i < 3:
            downs[i - 1].wait_recv()
            acc_down[i - 1] = s[ring_at[i - 3], :] + ring_down[i - 1]
            downs[i].start()

    def turn_a():
        for copy in first_a:
            copy.wait_recv()
        sa[...] = s[own_ya, :] + ra1[0] + ra1[1] + ra1[2]
        for copy in second_a:
            copy.start()

    for copy in [ups[0], downs[0]] + first_a:
        copy.start()
    for copy in across:
        copy.wait_recv()
    assemble(gf, w)
    factor(w, lefts, rights, {0: lambda: ring_step(1), 2: lambda: ring_step(2), 3: turn_a, 4: lambda: ring_step(3)})
    ups[-1].wait_recv()
    downs[-1].wait_recv()
    sb[...] = s[rows(half + zc * za, za), :] + ring_up[3] + ring_down[2]
    second_b = []
    for d in range(1, NY):
        t, dev = lk.at_y(d)
        second_b.append(cp.start(sb.at[rows(t * piece, piece)], rb2.at[d - 1], dev))
    for copy in second_b:
        copy.wait_recv()
    left_b = sb[rows(lk.y * piece, piece), :] + rb2[0] + rb2[1] + rb2[2]
    for copy in second_a:
        copy.wait_recv()
    left_a = sa[rows(zc * piece, piece), :]
    for i in range(NZ - 1):
        left_a = left_a + ra2[i]

    left = jnp.concatenate([left_a, left_b], axis=0)
    right = [times_inverse(left, w, k) for k in range(NBLK)]
    me1 = lk.z * 2 + lk.core
    me2 = lk.x * NY + lk.y
    base = lk.core * RANK
    at_a = rows16(base + lk.y * ya + zc * piece, piece)
    at_b = rows16(base + half + zc * za + lk.y * piece, piece)
    for k in range(NBLK):
        rounded = right[k].astype(BF16)

        @pl.when(owner)
        def _():
            nb[at_a, block(k)] = rounded[:piece]
            nb[at_b, block(k)] = rounded[piece:]

        sq1[me1, k:k + 1, :] = jnp.where(owner, jnp.sum(right[k] * right[k], axis=0, keepdims=True), 0.0)
    sq1[me1, NBLK:, :] = jnp.zeros((1, NB), F32)
    own = nb.at[at_b]
    gather_b = [cp.start(own, own, lk.at_y(d)[1], when=owner) for d in range(1, NY)]
    own = nb.at[at_a]
    gather_a = [cp.start(own, own, lk.at_z(d)[1], when=owner) for d in range(1, NZ)]
    squares = [cp.start(sq1.at[me1], sq1.at[me1], lk.at_zc(d)[1]) for d in range(1, 2 * NZ)]

    def owned(shift):
        return lax.rem(lk.z + NZ + shift, NZ) < OWN

    def part_b(shift):
        return nb.at[rows16(base + half + jnp.minimum(lax.rem(lk.z + NZ + shift, NZ), OWN - 1) * za, za)]

    @pl.when(owner)
    def _():
        for copy in gather_b:
            copy.wait_recv()

    ups = [cp.start(part_b(0), part_b(0), up, when=owned(0))]
    downs = [cp.start(part_b(0), part_b(0), down, when=owned(0))]

    def gather_step(i):
        pl.when(owned(-i))(ups[-1].wait_recv)
        ups.append(cp.start(part_b(-i), part_b(-i), up, when=owned(-i)))
        if i < 3:
            pl.when(owned(i))(downs[-1].wait_recv)
            downs.append(cp.start(part_b(i), part_b(i), down, when=owned(i)))

    for d in range(1, NZ):
        pl.when(owned(-d))(gather_a[d - 1].wait_recv)
    own = nb.at[rows16(base + lk.y * ya, ya)]
    gather_a = [cp.start(own, own, lk.at_y(d)[1]) for d in range(1, NY)]
    for copy in squares:
        copy.wait_recv()
    total = sq1[0]
    for i in range(1, 2 * NZ):
        total = total + sq1[i]
    sq2[me2] = total
    squares = [cp.start(sq2.at[me2], sq2.at[me2], lk.at_xy(dx, dy)[1])
               for dx in range(NX) for dy in range(NY) if dx or dy]
    gather_step(1)
    for k in range(4):
        xf[:, block(k)] = times_inverse(pf[...], w, k)
    gather_step(2)
    for k in range(4, 6):
        xf[:, block(k)] = times_inverse(pf[...], w, k)
    gather_step(3)
    for k in range(6, NBLK):
        xf[:, block(k)] = times_inverse(pf[...], w, k)
    for copy in gather_a:
        copy.wait_recv()
    own = nb.at[rows16(base, half)]
    across = [cp.start(own, own, core_dev)]
    for copy in squares:
        copy.wait_recv()
    total = sq2[0]
    for i in range(1, NX * NY):
        total = total + sq2[i]
    rms = jnp.sqrt(total / COLS_D + EPS)
    for k in range(NBLK):
        ortho = xf[:, block(k)]
        low_out[:n, block(k)] = (ortho * rms[k:k + 1, :]).astype(BF16)
        low_out[n:, block(k)] = ortho.astype(BF16)
    pl.when(owned(-4))(ups[-1].wait_recv)
    pl.when(owned(3))(downs[-1].wait_recv)
    own = nb.at[rows16(base + half, half)]
    across.append(cp.start(own, own, core_dev))
    scale = 1.0 / rms

    def normalize(start, size):
        at = rows16(start, size)
        for k in range(NBLK):
            nb_out[at, block(k)] = (nb[at, block(k)].astype(F32) * scale[k:k + 1, :]).astype(BF16)

    normalize(base, RANK)
    for i, copy in enumerate(across):
        copy.wait_recv()
        normalize((1 - lk.core) * RANK + i * half, half)
    cp.finish()


def rows16(start, size):
    return pl.ds(pl.multiple_of(start, 16), size)


def dion(momentum, gradient, basis):
    n, columns = momentum.shape
    vm = pl.BlockSpec(memory_space=pltpu.VMEM)
    half, big, small = RANK // 2, RANK // 4, RANK // 16
    ya, za, piece = half // NY, half // OWN, half // NY // OWN

    def buffer(*shape, dtype=F32):
        return pltpu.VMEM(shape, dtype)

    return pl.pallas_call(
        step_kernel,
        out_shape=(jax.ShapeDtypeStruct((2 * n, RANK), BF16), jax.ShapeDtypeStruct((columns, RANK), BF16)),
        in_specs=[pl.BlockSpec(memory_space=pl.ANY)] * 3,
        out_specs=(vm, vm),
        scratch_shapes=[
            buffer(n, RANK), buffer(3, n // NX, RANK), buffer(2 * n // NX, RANK + 3 * NB), buffer(n, RANK),
            buffer(2, RANK, NB), buffer(2, 3, big, NB), buffer(2, big, NB), buffer(2, 3, small, NB),
            buffer(2, small, NB), buffer(small, NB), buffer(4, small, NB), buffer(2, small, NB),
            buffer(2, big, NB), buffer(2, 2, RANK, NB), buffer(n, columns, dtype=BF16),
            buffer(RANK, RANK), buffer(RANK, RANK), buffer(RANK, RANK), buffer(RANK + NB, RANK),
            buffer(NY - 1, ya, RANK), buffer(ya, RANK), buffer(NZ - 1, piece, RANK),
            buffer(4, za, RANK), buffer(3, za, RANK), buffer(3, za, RANK), buffer(2, za, RANK),
            buffer(za, RANK), buffer(NY - 1, piece, RANK),
            buffer(2 * NZ, 8, NB), buffer(NX * NY, 8, NB), buffer(columns, RANK, dtype=BF16),
            buffer(n, RANK),
            buffer(6 * NB, RANK + NB, dtype=BF16), buffer(6 * NB, RANK, dtype=BF16),
            buffer(n, columns), buffer(n, columns, dtype=BF16), buffer(columns, RANK, dtype=BF16),
            pltpu.SemaphoreType.DMA((3,)),
            pltpu.SemaphoreType.DMA((COPIES,)), pltpu.SemaphoreType.DMA((COPIES,)),
        ],
        compiler_params=pltpu.CompilerParams(
            collective_id=0, has_side_effects=True, vmem_limit_bytes=60 * 2**20),
    )(momentum, gradient, basis)


def close_kernel(low, basis, mom, grad, mom_out, update_out, basis_out):
    n = mom.shape[0]
    products = lax.dot_general(low[...], basis[...], (((1,), (1,)), ((), ())), preferred_element_type=F32)
    mom_out[...] = mom[...] + grad[...].astype(F32) - (1.0 - DECAY) * products[:n]
    update_out[...] = (math.sqrt(ROWS_FF / RANK) * products[n:]).astype(BF16)
    basis_out[...] = basis[...]


def close(low, basis, momentum, gradient):
    n, columns = momentum.shape
    width = 2 * NB
    across = pl.BlockSpec((n, width), lambda j: (0, j))
    along = pl.BlockSpec((width, RANK), lambda j: (j, 0))
    return pl.pallas_call(
        close_kernel,
        grid=(columns // width,),
        in_specs=[pl.BlockSpec((2 * n, RANK), lambda j: (0, 0)), along, across, across],
        out_specs=(across, across, along),
        out_shape=(jax.ShapeDtypeStruct((n, columns), F32), jax.ShapeDtypeStruct((n, columns), BF16),
                   jax.ShapeDtypeStruct((columns, RANK), BF16)),
        compiler_params=pltpu.CompilerParams(vmem_limit_bytes=32 * 2**20),
    )(low, basis, momentum, gradient)


def body(momentum, gradient, column_basis):
    low, new_basis = dion(momentum, gradient, column_basis)
    return close(low, new_basis, momentum, gradient)


def solution(mesh):
    placed = (P("fsdp", "tp"), P("fsdp", "tp"), P("tp", None))
    return jax.shard_map(
        body,
        mesh=mesh,
        in_specs=placed,
        out_specs=(P("fsdp", "tp"), P("fsdp", "tp"), P("tp", None)),
        check_vma=False,
    )
```

time: 979 us -> 152 us (0.16)
  waiting for transfers between devices: 321 us -> 0 us
  other arithmetic: 246 us -> 0 us
  blocking collectives: 228 us -> 0 us
  Pallas kernels: 0 us -> 148 us
  local copies, waits for them, and re-layouts: 70.4 us -> 3.13 us
  matrix products: 57.7 us -> 0 us
  starting transfers between devices: 28.8 us -> 0 us
  between operations: 19.4 us -> 0.68 us
    psum x2 -> x0, waiting for transfers between devices: 246 us -> none  [the longest x1 193 us: body(): summed = lax.psum(gram_payload(projected), 'fsdp')]
    another operation x29 -> x0, other arithmetic: 232 us -> none  [the longest x26 157 us: body(): lower_factor = jnp.linalg.cholesky(gram_matrix(summed, rank_size))]
    unnamed x1 -> x0, blocking collectives: 150 us -> none
    pallas_call x0 -> x2, Pallas kernels: none -> 148 us  [the longest x1 142 us: dion(): pl.pallas_call(step_kernel, out_shape=(jax.ShapeDtypeStruct((2 * n, RANK)...]
    psum x1 -> x0, blocking collectives: 78 us -> none  [body(): lax.psum(jnp.sum(right_factor * right_factor, axis=0), ('fsdp', 'tp'))]
    all_gather x1 -> x0, waiting for transfers between devices: 74.5 us -> none  [body(): new_basis = lax.all_gather(basis_piece, 'fsdp', axis=0, tiled=True)]
    another operation x58 -> x0, local copies, waits for them, and re-layouts: 35.9 us -> none
    another operation x25 -> x0, matrix products: 35.4 us -> none  [the longest x12 21.4 us: body(): lower_factor = jnp.linalg.cholesky(gram_matrix(summed, rank_size))]
  transfers between devices with their start and end apart: 11 -> 0, of which waited for: 3 -> 0; matrix products, arithmetic and copies ran while one was open for 0% -> 0% of each run, Pallas kernels for 0% -> 0%
where the time goes in v2:
time: 152 us
  Pallas kernels  148 us (97%)
  local copies, waits for them, and re-layouts  3.13 us (2%)
    pallas_call x1, Pallas kernels, dion(): pl.pallas_call(step_kernel, out_shape=(jax.ShapeDtypeStruct((2 * n, RANK)...  142 us
    pallas_call x1, Pallas kernels, close(): pl.pallas_call(close_kernel, grid=(columns // width,), in_specs=[pl.Block...  5.53 us
    unnamed x8, local copies, waits for them, and re-layouts  3.13 us

profile of v2, /device:TPU:1, one launch (start us, length us, event | category | flops | bytes accessed | tf_op | source)
XLA Modules:
  0.0 151.5 jit_solution(12973490481482971226)
XLA Ops:
  0.6 0.0 copy-start.1
  0.6 0.0 copy-start
  0.7 142.2 %shard_map.58 = (bf16[576,896]{1,0:T(8,128)(2,1)}, bf16[1792,896]{1,0:T(8,128)(2,1)}) custom-call(f32[288,1792]{1,0:T(8,128)} %mom.1, bf16[288,1792]{1,0:T(8,128)(2,1)} %grad.1, bf16[1792,896]{1,0:T(8,128)(2,1)} %basis_any.1), custom_call_target="tpu_custom_call" | custom-call | tf_op jit(solution)/shard_map/pallas_call | solution.py:552
  142.8 0.0 copy-done.1
  142.8 0.0 copy-done
  142.9 0.0 copy-start.2
  142.9 1.9 %copy-done.2 = bf16[1792,896]{1,0:T(8,128)(2,1)S(1)} copy-done((bf16[1792,896]{1,0:T(8,128)(2,1)S(1)}, bf16[1792,896]{1,0:T(8,128)(2,1)}, u32[]{:S(2)}) %copy-start.2) | copy-done | bytes 3211288
  144.8 0.0 copy-start.3
  144.8 1.2 copy-done.3
  146.0 5.5 %shard_map.59 = (f32[288,1792]{1,0:T(8,128)}, bf16[288,1792]{1,0:T(8,128)(2,1)}, bf16[1792,896]{1,0:T(8,128)(2,1)}) custom-call(bf16[576,896]{1,0:T(8,128)(2,1)S(1)} %copy-done.3, bf16[1792,896]{1,0:T(8,128)(2,1)S(1)} %copy-done.2, f32[288,1792]{1,0:T(8,128)S(1)} %copy-done, bf16[288,1792]{1,0:T(8,128)(2,1)S(1)} %copy-done.1), custom_call_target="tpu_custom_call" | custom-call | tf_op jit(solution)/shard_map/pallas_call | solution.py:591
Async XLA Ops:
  0.6 142.2 %copy-start.1 = (bf16[288,1792]{1,0:T(8,128)(2,1)S(1)}, bf16[288,1792]{1,0:T(8,128)(2,1)}, u32[]{:S(2)}) copy-start(bf16[288,1792]{1,0:T(8,128)(2,1)} %grad.1) | copy-start | bytes 3096580
  0.6 142.2 %copy-start = (f32[288,1792]{1,0:T(8,128)S(1)}, f32[288,1792]{1,0:T(8,128)}, u32[]{:S(2)}) copy-start(f32[288,1792]{1,0:T(8,128)} %mom.1) | copy-start | bytes 6193156
  142.9 1.9 %copy-start.2 = (bf16[1792,896]{1,0:T(8,128)(2,1)S(1)}, bf16[1792,896]{1,0:T(8,128)(2,1)}, u32[]{:S(2)}) copy-start(bf16[1792,896]{1,0:T(8,128)(2,1)} %get-tuple-element.6.basis) | copy-start | bytes 9633796
  144.8 1.2 copy-start.3

commit v3 on v2

--- a/solution.py
+++ b/solution.py
@@ -198,10 +198,18 @@
                 w[c * NB:(c + 1) * NB, b * NB:(b + 1) * NB] = block.T
 
 
+def two(x):
+    high = x.astype(BF16)
+    return high, (x - high.astype(F32)).astype(BF16)
+
+
 def times_inverse(left, w, k):
     n = (k + 1) * NB
+    high, low = two(left[:, :n])
+    w_high, w_low = two(w[k * NB:n, :n])
     return lax.dot_general(
-        left[:, :n], w[k * NB:n, :n], (((1,), (1,)), ((), ())), precision=HI, preferred_element_type=F32)
+        jnp.concatenate([high, high, low], axis=1), jnp.concatenate([w_high, w_low, w_high], axis=1),
+        (((1,), (1,)), ((), ())), preferred_element_type=F32)
 
 
 def block(i):
@@ -224,7 +232,7 @@
     return (high, mid, high, low, high, mid), (high, high, mid, high, low, mid)
 
 
-def factor(w, lefts, rights, beside):
+def factor(w, lefts, rights, amid, beside):
     w[pl.ds(RANK, NB), :] = jnp.zeros((NB, RANK), F32)
     lefts[:, pl.ds(RANK, NB)] = jnp.zeros((6 * NB, NB), BF16)
 
@@ -233,6 +241,8 @@
         at = pl.ds(o, NB)
         inv = jnp.concatenate(
             factor128([w[pl.ds(pl.multiple_of(o + 8 * t, 8), 8), at] for t in range(16)]), axis=0)
+        for when, act in amid.items():
+            pl.when(k == when)(act)
         left = jnp.concatenate(terms(inv)[0], axis=1)
         right = jnp.concatenate(terms(w[at, :])[1], axis=0)
         w[at, :] = jnp.dot(left, right, preferred_element_type=F32)
@@ -417,19 +427,26 @@
         for copy in second_a:
             copy.start()
 
+    second_b = []
+    for d in range(1, NY):
+        t, dev = lk.at_y(d)
+        second_b.append(cp.make(sb.at[rows(t * piece, piece)], rb2.at[d - 1], dev))
+    own_za = rows(half + zc * za, za)
+
+    def turn_b():
+        ups[3].wait_recv()
+        downs[2].wait_recv()
+        sb[...] = s[own_za, :] + ring_up[3] + ring_down[2]
+        for copy in second_b:
+            copy.start()
+
     for copy in [ups[0], downs[0]] + first_a:
         copy.start()
     for copy in across:
         copy.wait_recv()
     assemble(gf, w)
-    factor(w, lefts, rights, {0: lambda: ring_step(1), 2: lambda: ring_step(2), 3: turn_a, 4: lambda: ring_step(3)})
-    ups[-1].wait_recv()
-    downs[-1].wait_recv()
-    sb[...] = s[rows(half + zc * za, za), :] + ring_up[3] + ring_down[2]
-    second_b = []
-    for d in range(1, NY):
-        t, dev = lk.at_y(d)
-        second_b.append(cp.start(sb.at[rows(t * piece, piece)], rb2.at[d - 1], dev))
+    factor(w, lefts, rights, {3: turn_a},
+           {0: lambda: ring_step(1), 1: lambda: ring_step(2), 2: lambda: ring_step(3), 5: turn_b})
     for copy in second_b:
         copy.wait_recv()
     left_b = sb[rows(lk.y * piece, piece), :] + rb2[0] + rb2[1] + rb2[2]
@@ -483,6 +500,12 @@
             pl.when(owned(i))(downs[-1].wait_recv)
             downs.append(cp.start(part_b(i), part_b(i), down, when=owned(i)))
 
+    def ortho(first, last):
+        for k in range(first, last):
+            xf[:, block(k)] = times_inverse(pf[...], w, k)
+
+    ortho(0, 4)
+    gather_step(1)
     for d in range(1, NZ):
         pl.when(owned(-d))(gather_a[d - 1].wait_recv)
     own = nb.at[rows16(base + lk.y * ya, ya)]
@@ -495,19 +518,10 @@
     sq2[me2] = total
     squares = [cp.start(sq2.at[me2], sq2.at[me2], lk.at_xy(dx, dy)[1])
                for dx in range(NX) for dy in range(NY) if dx or dy]
-    gather_step(1)
-    for k in range(4):
-        xf[:, block(k)] = times_inverse(pf[...], w, k)
+    ortho(4, 6)
     gather_step(2)
-    for k in range(4, 6):
-        xf[:, block(k)] = times_inverse(pf[...], w, k)
+    ortho(6, NBLK)
     gather_step(3)
-    for k in range(6, NBLK):
-        xf[:, block(k)] = times_inverse(pf[...], w, k)
-    for copy in gather_a:
-        copy.wait_recv()
-    own = nb.at[rows16(base, half)]
-    across = [cp.start(own, own, core_dev)]
     for copy in squares:
         copy.wait_recv()
     total = sq2[0]
@@ -515,21 +529,25 @@
         total = total + sq2[i]
     rms = jnp.sqrt(total / COLS_D + EPS)
     for k in range(NBLK):
-        ortho = xf[:, block(k)]
-        low_out[:n, block(k)] = (ortho * rms[k:k + 1, :]).astype(BF16)
-        low_out[n:, block(k)] = ortho.astype(BF16)
+        low_out[:n, block(k)] = (xf[:, block(k)] * rms[k:k + 1, :]).astype(BF16)
+        low_out[n:, block(k)] = xf[:, block(k)].astype(BF16)
+    for copy in gather_a:
+        copy.wait_recv()
+    own = nb.at[rows16(base, half)]
+    across = [cp.start(own, own, core_dev)]
+    scale = 1.0 / rms
+
+    def normalize(start, size):
+        at = rows16(start, size)
+        for k in range(NBLK):
+            nb_out[at, block(k)] = (nb[at, block(k)].astype(F32) * scale[k:k + 1, :]).astype(BF16)
+
+    normalize(base, half)
     pl.when(owned(-4))(ups[-1].wait_recv)
     pl.when(owned(3))(downs[-1].wait_recv)
     own = nb.at[rows16(base + half, half)]
     across.append(cp.start(own, own, core_dev))
-    scale = 1.0 / rms
-
-    def normalize(start, size):
-        at = rows16(start, size)
-        for k in range(NBLK):
-            nb_out[at, block(k)] = (nb[at, block(k)].astype(F32) * scale[k:k + 1, :]).astype(BF16)
-
-    normalize(base, RANK)
+    normalize(base + half, half)
     for i, copy in enumerate(across):
         copy.wait_recv()
         normalize((1 - lk.core) * RANK + i * half, half)
@@ -595,7 +613,7 @@
         out_specs=(across, across, along),
         out_shape=(jax.ShapeDtypeStruct((n, columns), F32), jax.ShapeDtypeStruct((n, columns), BF16),
                    jax.ShapeDtypeStruct((columns, RANK), BF16)),
-        compiler_params=pltpu.CompilerParams(vmem_limit_bytes=32 * 2**20),
+        compiler_params=pltpu.CompilerParams(vmem_limit_bytes=60 * 2**20),
     )(low, basis, momentum, gradient)
 
 

time: 152 us -> 145 us (0.954)
  Pallas kernels: 148 us -> 144 us
  local copies, waits for them, and re-layouts: 3.13 us -> 0 us
    pallas_call x1, Pallas kernels: 142 us -> 134 us  [dion(): pl.pallas_call(step_kernel, out_shape=(jax.ShapeDtypeStruct((2 * n, RANK)...]
    pallas_call x1, Pallas kernels: 5.53 us -> 9.15 us  [close(): pl.pallas_call(close_kernel, grid=(columns // width,), in_specs=[pl.Block...]
    unnamed x8 -> x0, local copies, waits for them, and re-layouts: 3.13 us -> none
where the time goes in v3:
time: 145 us; the launch traced here: 144 us
  Pallas kernels  144 us (99%)
    pallas_call x1, Pallas kernels, dion(): pl.pallas_call(step_kernel, out_shape=(jax.ShapeDtypeStruct((2 * n, RANK)...  134 us
    pallas_call x1, Pallas kernels, close(): pl.pallas_call(close_kernel, grid=(columns // width,), in_specs=[pl.Block...  9.15 us

profile of v3, /device:TPU:1, one launch (start us, length us, event | category | flops | bytes accessed | tf_op | source)
XLA Modules:
  0.0 144.3 jit_solution(17374408867342167810)
XLA Ops:
  0.6 134.5 %shard_map.58 = (bf16[576,896]{1,0:T(8,128)(2,1)}, bf16[1792,896]{1,0:T(8,128)(2,1)}) custom-call(f32[288,1792]{1,0:T(8,128)} %mom.1, bf16[288,1792]{1,0:T(8,128)(2,1)} %grad.1, bf16[1792,896]{1,0:T(8,128)(2,1)} %basis_any.1), custom_call_target="tpu_custom_call" | custom-call | tf_op jit(solution)/shard_map/pallas_call | solution.py:570
  135.1 9.2 %shard_map.59 = (f32[288,1792]{1,0:T(8,128)}, bf16[288,1792]{1,0:T(8,128)(2,1)}, bf16[1792,896]{1,0:T(8,128)(2,1)}) custom-call(bf16[576,896]{1,0:T(8,128)(2,1)} %get-tuple-element.5.low, bf16[1792,896]{1,0:T(8,128)(2,1)} %get-tuple-element.6.basis, f32[288,1792]{1,0:T(8,128)} %mom.1, bf16[288,1792]{1,0:T(8,128)(2,1)} %grad.1), custom_call_target="tpu_custom_call" | custom-call | tf_op jit(solution)/shard_map/pallas_call | solution.py:609

commit v4 on v3

--- a/solution.py
+++ b/solution.py
@@ -268,12 +268,12 @@
 
 
 OWN = 7
-COPIES = 3 + 1 + 6 + 6 + 5 + 3 + 6 + 6 + 8 + 1 + 3 + 7 + 7 + 3 + 15 + 15 + 7 + 3 + 3 + 7 + 2
-
-
-def step_kernel(mom_any, grad_any, basis_any, low_out, nb_out, pp, prx, pc, pf, ga, r1, s1, r2, zin, zp, zr, zt, a4, gf, low,
+COPIES = 3 + 1 + 6 + 6 + 5 + 3 + 6 + 6 + 8 + 1 + 3 + 7 + 7 + 3 + 15 + 15 + 7 + 3 + 3 + 7 + 2 + 7
+
+
+def step_kernel(mom_any, grad_any, basis_any, low_any, nb_any, pp, prx, pc, pf, ga, r1, s1, r2, zin, zp, zr, zt, a4, gf, low,
                 so, sr, s, w, ra1, sa, ra2, ring_up, ring_down, acc_up, acc_down, sb, rb2, sq1, sq2, nb, xf,
-                lefts, rights, mom, grad, basis, in_sem, ssem, rsem):
+                lefts, rights, mom, grad, basis, low_out, nb_out, in_sem, out_sem, ssem, rsem):
     inputs = [pltpu.make_async_copy(src, dst, in_sem.at[i])
               for i, (src, dst) in enumerate(((mom_any, mom), (grad_any, grad), (basis_any, basis)))]
     for copy in inputs:
@@ -492,13 +492,22 @@
 
     ups = [cp.start(part_b(0), part_b(0), up, when=owned(0))]
     downs = [cp.start(part_b(0), part_b(0), down, when=owned(0))]
+    passed = []
+
+    def pass_on(shift):
+        piece_b = part_b(shift)
+        passed.append((cp.start(piece_b, piece_b, core_dev, when=owned(shift)), owned(shift)))
+
+    pass_on(0)
 
     def gather_step(i):
         pl.when(owned(-i))(ups[-1].wait_recv)
         ups.append(cp.start(part_b(-i), part_b(-i), up, when=owned(-i)))
+        pass_on(-i)
         if i < 3:
             pl.when(owned(i))(downs[-1].wait_recv)
             downs.append(cp.start(part_b(i), part_b(i), down, when=owned(i)))
+            pass_on(i)
 
     def ortho(first, last):
         for k in range(first, last):
@@ -531,6 +540,8 @@
     for k in range(NBLK):
         low_out[:n, block(k)] = (xf[:, block(k)] * rms[k:k + 1, :]).astype(BF16)
         low_out[n:, block(k)] = xf[:, block(k)].astype(BF16)
+    stores = [pltpu.make_async_copy(low_out, low_any, out_sem.at[4])]
+    stores[0].start()
     for copy in gather_a:
         copy.wait_recv()
     own = nb.at[rows16(base, half)]
@@ -541,16 +552,22 @@
         at = rows16(start, size)
         for k in range(NBLK):
             nb_out[at, block(k)] = (nb[at, block(k)].astype(F32) * scale[k:k + 1, :]).astype(BF16)
+        stores.append(pltpu.make_async_copy(nb_out.at[at], nb_any.at[at], out_sem.at[len(stores) - 1]))
+        stores[-1].start()
 
     normalize(base, half)
     pl.when(owned(-4))(ups[-1].wait_recv)
     pl.when(owned(3))(downs[-1].wait_recv)
-    own = nb.at[rows16(base + half, half)]
-    across.append(cp.start(own, own, core_dev))
+    pass_on(-4)
+    pass_on(3)
     normalize(base + half, half)
-    for i, copy in enumerate(across):
-        copy.wait_recv()
-        normalize((1 - lk.core) * RANK + i * half, half)
+    across[0].wait_recv()
+    normalize((1 - lk.core) * RANK, half)
+    for copy, arrives in passed:
+        pl.when(arrives)(copy.wait_recv)
+    normalize((1 - lk.core) * RANK + half, half)
+    for copy in stores:
+        copy.wait()
     cp.finish()
 
 
@@ -560,7 +577,6 @@
 
 def dion(momentum, gradient, basis):
     n, columns = momentum.shape
-    vm = pl.BlockSpec(memory_space=pltpu.VMEM)
     half, big, small = RANK // 2, RANK // 4, RANK // 16
     ya, za, piece = half // NY, half // OWN, half // NY // OWN
 
@@ -571,7 +587,7 @@
         step_kernel,
         out_shape=(jax.ShapeDtypeStruct((2 * n, RANK), BF16), jax.ShapeDtypeStruct((columns, RANK), BF16)),
         in_specs=[pl.BlockSpec(memory_space=pl.ANY)] * 3,
-        out_specs=(vm, vm),
+        out_specs=(pl.BlockSpec(memory_space=pl.ANY),) * 2,
         scratch_shapes=[
             buffer(n, RANK), buffer(3, n // NX, RANK), buffer(2 * n // NX, RANK + 3 * NB), buffer(n, RANK),
             buffer(2, RANK, NB), buffer(2, 3, big, NB), buffer(2, big, NB), buffer(2, 3, small, NB),
@@ -585,7 +601,8 @@
             buffer(n, RANK),
             buffer(6 * NB, RANK + NB, dtype=BF16), buffer(6 * NB, RANK, dtype=BF16),
             buffer(n, columns), buffer(n, columns, dtype=BF16), buffer(columns, RANK, dtype=BF16),
-            pltpu.SemaphoreType.DMA((3,)),
+            buffer(2 * n, RANK, dtype=BF16), buffer(columns, RANK, dtype=BF16),
+            pltpu.SemaphoreType.DMA((3,)), pltpu.SemaphoreType.DMA((5,)),
             pltpu.SemaphoreType.DMA((COPIES,)), pltpu.SemaphoreType.DMA((COPIES,)),
         ],
         compiler_params=pltpu.CompilerParams(
@@ -603,7 +620,7 @@
 
 def close(low, basis, momentum, gradient):
     n, columns = momentum.shape
-    width = 2 * NB
+    width = 7 * NB
     across = pl.BlockSpec((n, width), lambda j: (0, j))
     along = pl.BlockSpec((width, RANK), lambda j: (j, 0))
     return pl.pallas_call(

time: 145 us -> 141 us (0.972)
  Pallas kernels: 144 us -> 140 us
    pallas_call x1, Pallas kernels: 9.15 us -> 7.06 us  [close(): pl.pallas_call(close_kernel, grid=(columns // width,), in_specs=[pl.Block...]
    pallas_call x1, Pallas kernels: 134 us -> 133 us  [dion(): pl.pallas_call(step_kernel, out_shape=(jax.ShapeDtypeStruct((2 * n, RANK)...]
where the time goes in v4:
time: 141 us; the launch traced here: 140 us
  Pallas kernels  140 us (99%)
    pallas_call x1, Pallas kernels, dion(): pl.pallas_call(step_kernel, out_shape=(jax.ShapeDtypeStruct((2 * n, RANK)...  133 us
    pallas_call x1, Pallas kernels, close(): pl.pallas_call(close_kernel, grid=(columns // width,), in_specs=[pl.Block...  7.06 us

profile of v4, /device:TPU:1, one launch (start us, length us, event | category | flops | bytes accessed | tf_op | source)
XLA Modules:
  0.0 140.4 jit_solution(10478938759413809750)
XLA Ops:
  0.6 132.7 %shard_map.58 = (bf16[576,896]{1,0:T(8,128)(2,1)}, bf16[1792,896]{1,0:T(8,128)(2,1)}) custom-call(f32[288,1792]{1,0:T(8,128)} %mom.1, bf16[288,1792]{1,0:T(8,128)(2,1)} %grad.1, bf16[1792,896]{1,0:T(8,128)(2,1)} %basis_any.1), custom_call_target="tpu_custom_call" | custom-call | tf_op jit(solution)/shard_map/pallas_call | solution.py:586
  133.3 7.1 %shard_map.59 = (f32[288,1792]{1,0:T(8,128)}, bf16[288,1792]{1,0:T(8,128)(2,1)}, bf16[1792,896]{1,0:T(8,128)(2,1)}) custom-call(bf16[576,896]{1,0:T(8,128)(2,1)} %get-tuple-element.5.low, bf16[1792,896]{1,0:T(8,128)(2,1)} %get-tuple-element.6.basis, f32[288,1792]{1,0:T(8,128)} %mom.1, bf16[288,1792]{1,0:T(8,128)(2,1)} %grad.1), custom_call_target="tpu_custom_call" | custom-call | tf_op jit(solution)/shard_map/pallas_call | solution.py:626

commit v5 on v4

--- a/solution.py
+++ b/solution.py
@@ -112,8 +112,8 @@
     return pl.ds(pl.multiple_of(start, 8), size)
 
 
-def cross_half(low, projected, half):
-    lhs = low[:, pl.ds(pl.multiple_of(half * RANK, NB), RANK)]
+def cross_part(low, projected, half, part):
+    lhs = low[:, pl.ds(pl.multiple_of(half * RANK + part.start, NB), part.size)]
     p = projected[...]
     high = p.astype(BF16)
     rest = (p - high.astype(F32)).astype(BF16)
@@ -268,7 +268,7 @@
 
 
 OWN = 7
-COPIES = 3 + 1 + 6 + 6 + 5 + 3 + 6 + 6 + 8 + 1 + 3 + 7 + 7 + 3 + 15 + 15 + 7 + 3 + 3 + 7 + 2 + 7
+COPIES = 3 + 1 + 6 + 6 + 5 + 3 + 6 + 6 + 8 + 1 + 3 + 7 + 7 + 3 + 15 + 15 + 7 + 3 + 3 + 7 + 2 + 7 + 1
 
 
 def step_kernel(mom_any, grad_any, basis_any, low_any, nb_any, pp, prx, pc, pf, ga, r1, s1, r2, zin, zp, zr, zt, a4, gf, low,
@@ -378,15 +378,17 @@
     across = [cp.start(own0, own0, core_dev), cp.start(own1, own1, core_dev)]
     for copy in rest:
         copy.wait_recv()
-    so[...] = cross_half(low, pf, 1 - lk.core)
-    cross = cp.start(so, sr, core_dev)
-    s[...] = cross_half(low, pf, lk.core)
+    parts = (pl.ds(3 * NB, 4 * NB), pl.ds(0, 3 * NB))
+    cross = []
+    for at in parts:
+        so[at, :] = cross_part(low, pf, 1 - lk.core, at)
+        cross.append(cp.start(so.at[at], sr.at[at], core_dev))
+    for at in parts:
+        s[at, :] = cross_part(low, pf, lk.core, at)
     for copy, h, t in sent:
         copy.wait_recv()
         piece = gf.at[lk.core, h, rows(t * big, big)]
         across.append(cp.start(piece, piece, core_dev))
-    cross.wait_recv()
-    s[...] += sr[...]
 
     half = RANK // 2
     ya, za, piece = half // NY, half // OWN, half // NY // OWN
@@ -440,8 +442,11 @@
         for copy in second_b:
             copy.start()
 
-    for copy in [ups[0], downs[0]] + first_a:
-        copy.start()
+    for at, copy, ready in zip(parts, cross, ([ups[0], downs[0]], first_a)):
+        copy.wait_recv()
+        s[at, :] += sr[at, :]
+        for after in ready:
+            after.start()
     for copy in across:
         copy.wait_recv()
     assemble(gf, w)

time: 141 us -> 141 us (level)
  no operation moved by 1% of the time
where the time goes in v5:
time: 141 us
  Pallas kernels  140 us (99%)
    pallas_call x1, Pallas kernels, dion(): pl.pallas_call(step_kernel, out_shape=(jax.ShapeDtypeStruct((2 * n, RANK)...  133 us
    pallas_call x1, Pallas kernels, close(): pl.pallas_call(close_kernel, grid=(columns // width,), in_specs=[pl.Block...  7.06 us

profile of v5, /device:TPU:1, one launch (start us, length us, event | category | flops | bytes accessed | tf_op | source)
XLA Modules:
  0.0 140.8 jit_solution(6326251585952577351)
XLA Ops:
  0.6 133.1 %shard_map.58 = (bf16[576,896]{1,0:T(8,128)(2,1)}, bf16[1792,896]{1,0:T(8,128)(2,1)}) custom-call(f32[288,1792]{1,0:T(8,128)} %mom.1, bf16[288,1792]{1,0:T(8,128)(2,1)} %grad.1, bf16[1792,896]{1,0:T(8,128)(2,1)} %basis_any.1), custom_call_target="tpu_custom_call" | custom-call | tf_op jit(solution)/shard_map/pallas_call | solution.py:591
  133.7 7.1 %shard_map.59 = (f32[288,1792]{1,0:T(8,128)}, bf16[288,1792]{1,0:T(8,128)(2,1)}, bf16[1792,896]{1,0:T(8,128)(2,1)}) custom-call(bf16[576,896]{1,0:T(8,128)(2,1)} %get-tuple-element.5.low, bf16[1792,896]{1,0:T(8,128)(2,1)} %get-tuple-element.6.basis, f32[288,1792]{1,0:T(8,128)} %mom.1, bf16[288,1792]{1,0:T(8,128)(2,1)} %grad.1), custom_call_target="tpu_custom_call" | custom-call | tf_op jit(solution)/shard_map/pallas_call | solution.py:631
